TPU v7x, 512 devices: a whole 4x8x8 slice. The times are simulated.
512 devices in a mesh: azi: 64 (over y, z_lo, core), rad: 2 (over z_hi), batch: 4 (over x).
Axes of the slice: x: 4, y: 8, z: 8 (z_hi: 2, z_lo: 4; z = z_hi * 4 + z_lo), core: 2. Of those that a mesh axis runs over, the one named last changes fastest.
Arguments:
- snapshots: bfloat16 [4, 1024, 256, 256], P('batch', 'azi', 'rad'), may hold values from -6 to 6
- first_kernel: bfloat16 [9, 256, 256], P(None, None, 'batch'), may hold values from -0.125 to 0.125
- second_kernel: bfloat16 [9, 256, 256], P(None, None, 'batch'), may hold values from -0.125 to 0.125
- cotangent: bfloat16 [4, 512, 128, 256], P('batch', 'azi', 'rad'), may hold values from -16 to 16
Outputs:
- encoded: bfloat16 [4, 512, 128, 256], P('batch', 'azi', 'rad')
- input_grad: bfloat16 [4, 1024, 256, 256], P('batch', 'azi', 'rad')
- kernel_grad: float32 [589824], P(('azi', 'rad', 'batch'))
All inputs are finite; a program needn't handle non-finite values.
Results may differ from a plain program's by a relative error of at most 0.0095.
Values may be sent and summed in bfloat16 or wider, within the bound.
A program may use at most 64 MiB of HBM per device.

v0:
```python
import math

import jax
import jax.numpy as jnp
from jax import lax
from jax.sharding import PartitionSpec as P


def shifted(value, axis, steps):
    count = lax.axis_size(axis)
    pairs = [(source, (source + steps) % count) for source in range(count)]
    return lax.ppermute(value, axis, pairs)


def passed_along(x, axis, by):
    devices = lax.axis_size(axis)
    pairs = [(i, i + by) for i in range(devices) if 0 <= i + by < devices]
    return lax.ppermute(x, axis, pairs)


def padded(block, sides, width):
    for axis, dim in sides:
        count = lax.axis_size(axis)
        forward = [(i, i + 1) for i in range(count - 1)]
        forward.append((count - 1, 0))
        backward = [(target, source) for source, target in forward]
        low = lax.ppermute(
            lax.slice_in_dim(block, block.shape[dim] - width, None, axis=dim), axis, forward
        )
        high = lax.ppermute(lax.slice_in_dim(block, 0, width, axis=dim), axis, backward)
        block = jnp.concatenate([low, block, high], axis=dim)
    return block


def silu_slope(pre_act):
    sigmoid = jax.nn.sigmoid(pre_act)
    return sigmoid * (1.0 + pre_act * (1.0 - sigmoid))


def tap_conv(extended, weights, taps, stride, rows_out, cols_out, transpose):
    channels = extended.shape[-1]
    summed = jnp.zeros((rows_out * cols_out, channels), jnp.float32)
    for row_at, col_at, tap in taps:
        window = extended[
            row_at : row_at + stride * rows_out : stride,
            col_at : col_at + stride * cols_out : stride,
            :,
        ]
        window = window.reshape(rows_out * cols_out, channels)
        kernel = weights[tap].T if transpose else weights[tap]
        summed = summed + jnp.dot(window, kernel, preferred_element_type=jnp.float32)
    return summed.reshape(rows_out, cols_out, channels)


def parity_grad(grad_next, first_full, rows_out, cols_out):
    parity_taps = ([(1, 0)], [(2, 0), (0, 1)])
    channels = grad_next.shape[-1]
    row_list = []
    for row_parity in (0, 1):
        col_list = []
        for col_parity in (0, 1):
            taps = [
                (row_shift, col_shift, 3 * m + n)
                for m, row_shift in parity_taps[row_parity]
                for n, col_shift in parity_taps[col_parity]
            ]
            col_list.append(tap_conv(grad_next, first_full, taps, 1, rows_out, cols_out, True))
        row_list.append(jnp.stack(col_list, axis=2))
    stacked = jnp.stack(row_list, axis=1)
    return stacked.reshape(2 * rows_out, 2 * cols_out, channels)


def kernel_terms(act_ext, cot, rows_out, cols_out):
    channels = cot.shape[-1]
    flat_cot = cot.reshape(rows_out * cols_out, channels)
    terms = []
    for m in range(3):
        for n in range(3):
            window = act_ext[4 * m : 4 * m + rows_out, 4 * n : 4 * n + cols_out, :].reshape(
                rows_out * cols_out, channels
            )
            terms.append(
                lax.dot_general(
                    window, flat_cot, (((0,), (0,)), ((), ())), preferred_element_type=jnp.float32
                )
            )
    return jnp.stack(terms)


def attach_rims(field, direction):
    if direction == 1:
        edge_row = field[-1:]
    else:
        edge_row = field[:1]
    row_in = shifted(edge_row, "azi", direction)
    if direction == 1:
        widened = jnp.concatenate([row_in, field], 0)
        edge_col = widened[:, -1:]
    else:
        widened = jnp.concatenate([field, row_in], 0)
        edge_col = widened[:, :1]
    col_in = passed_along(edge_col, "rad", direction)
    if direction == 1:
        return jnp.concatenate([col_in, widened], 1)
    return jnp.concatenate([widened, col_in], 1)


def dilate_ext(field):
    extended = padded(field, (("azi", 0), ("rad", 1)), 4)
    cols_out = field.shape[1]
    column = lax.broadcasted_iota(jnp.int32, (1, cols_out + 8, 1), 1)
    band_index = lax.axis_index("rad")
    band_last = lax.axis_size("rad") - 1
    lower_out = jnp.logical_and(column < 4, band_index == 0)
    upper_out = jnp.logical_and(column >= cols_out + 4, band_index == band_last)
    inside = jnp.logical_not(jnp.logical_or(lower_out, upper_out))
    return jnp.where(inside, extended, jnp.zeros_like(extended))


def body(snapshots, first_kernel, second_kernel, cotangent):
    first_full, second_full = (
        lax.all_gather(first_kernel, "batch", axis=2, tiled=True),
        lax.all_gather(second_kernel, "batch", axis=2, tiled=True),
    )
    field = snapshots[0]
    cot = cotangent[0]
    rows_out = field.shape[0] // 2
    cols_out = field.shape[1] // 2
    stride_taps = [(m, n, 3 * m + n) for m in range(3) for n in range(3)]
    ahead_taps = [(4 * m, 4 * n, 3 * m + n) for m in range(3) for n in range(3)]
    back_taps = [(8 - 4 * m, 8 - 4 * n, 3 * m + n) for m in range(3) for n in range(3)]
    extended = attach_rims(field, 1)
    pre_act = tap_conv(extended, first_full, stride_taps, 2, rows_out, cols_out, False)
    activation = jax.nn.silu(pre_act).astype(jnp.bfloat16)
    act_ext = dilate_ext(activation)
    mixed_out = tap_conv(act_ext, second_full, ahead_taps, 1, rows_out, cols_out, False)
    encoded = (activation.astype(jnp.float32) + mixed_out).astype(jnp.bfloat16)
    grad_ext = dilate_ext(cot)
    grad_act = cot.astype(jnp.float32) + tap_conv(
        grad_ext, second_full, back_taps, 1, rows_out, cols_out, True
    )
    grad_pre = (grad_act * silu_slope(pre_act)).astype(jnp.bfloat16)
    flat_grad = kernel_terms(act_ext, cot, rows_out, cols_out)
    devices_all = lax.axis_size("azi") * lax.axis_size("rad") * lax.axis_size("batch")
    cells_all = devices_all * rows_out * cols_out
    flat_grad = (flat_grad * (1.0 / math.sqrt(cells_all))).reshape(-1)
    kernel_grad = lax.psum_scatter(
        flat_grad, ("azi", "rad", "batch"), scatter_dimension=0, tiled=True
    )
    grad_next = attach_rims(grad_pre, -1)
    input_grad = parity_grad(grad_next, first_full, rows_out, cols_out).astype(jnp.bfloat16)
    return (encoded[None], input_grad[None], kernel_grad)


def solution(mesh):
    return jax.shard_map(
        body,
        mesh=mesh,
        in_specs=(
            P("batch", "azi", "rad", None),
            P(None, None, "batch"),
            P(None, None, "batch"),
            P("batch", "azi", "rad", None),
        ),
        out_specs=(
            P("batch", "azi", "rad", None),
            P("batch", "azi", "rad", None),
            P(("azi", "rad", "batch")),
        ),
        check_vma=False,
    )
```

profile of v0, /device:TPU:1, one launch (start us, length us, event | category | flops | bytes accessed | tf_op | source)
XLA Modules:
  0.0 419.5 jit_solution(14264928126768241251)
XLA Ops:
  7.2 0.7 all-gather.3.cloned.1.call-update
  8.0 1.6 slice_bitcast_fusion.18
  9.6 8.8 %collective-permute-start.7 = (bf16[4,64,256]{2,1,0:T(8,128)(2,1)}, bf16[4,64,256]{2,1,0:T(8,128)(2,1)S(1)}, u32[]{:S(2)}, u32[]{:S(2)}) collective-permute-start(bf16[4,64,256]{2,1,0:T(8,128)(2,1)} %get-tuple-element.30), channel_id=1, source_target_pairs={{8,0},{16,8},{24,16},{32,24},{40,32},{48,40},{56,48},{64,56},{72,6... | collective-permute-start | bytes 393224 | tf_op jit(solution)/shard_map/ppermute | solution.py:30
  18.4 1.9 collective-permute-start.6
  20.4 0.8 slice_bitcast_fusion.53
  21.2 1.9 collective-permute-start
  23.2 2.7 slice.229
  25.8 2.7 slice.231
  28.5 2.7 slice.235
  31.2 2.7 slice.237
  34.9 6.8 %collective-permute-start.1 = (bf16[17,1,256]{2,1,0:T(2,128)(2,1)S(1)}, bf16[17,1,256]{2,1,0:T(2,128)(2,1)S(1)}, u32[]{:S(2)}, u32[]{:S(2)}) collective-permute-start(bf16[17,1,256]{2,1,0:T(2,128)(2,1)S(1)} %fusion.27), channel_id=1, source_target_pairs={{0,4},{1,5},{2,6},{3,7},{8,12},{9,13},{10,14},{11,15},{16,20},{17,... | collective-permute-start | bytes 26120 | tf_op jit(solution)/shard_map/ppermute | solution.py:18
  41.8 1.9 collective-permute-start.9
  43.7 7.3 %collective-permute-start.8 = (bf16[16,4,256]{2,1,0:T(4,128)(2,1)S(1)}, bf16[16,4,256]{2,1,0:T(4,128)(2,1)S(1)}, u32[]{:S(2)}, u32[]{:S(2)}) collective-permute-start(bf16[16,4,256]{2,1,0:T(4,128)(2,1)S(1)} %get-tuple-element.23), channel_id=1, source_target_pairs={{0,4},{4,0},{1,5},{5,1},{2,6},{6,2},{3,7},{7,3},{8,12},{12,8},{9,1... | collective-permute-start | bytes 98312 | tf_op jit(solution)/shard_map/ppermute | solution.py:27
  51.0 0.5 maximum_maximum_fusion
  51.6 0.4 slice.227
  52.0 2.7 slice.221
  54.7 2.7 slice.233
  57.4 0.4 maximum_select_fusion.1
  57.8 1.3 fusion.28
  59.1 1.2 fusion.19
  60.3 1.2 fusion.18
  61.4 15.4 %all-gather.5.cloned.1.call-done = bf16[9,256,256]{1,2,0:T(8,128)(2,1)} async-done(((bf16[9,256,64]{1,2,0:T(8,128)(2,1)}), bf16[9,256,256]{1,2,0:T(8,128)(2,1)}) %all-gather.5.cloned.1.call-update) | async-done | bytes 1179664 | tf_op jit(solution)/shard_map/all_gather | solution.py:123
  76.9 1.2 fusion.23
  78.1 1.2 convolution_add_fusion.11
  79.9 0.5 copy-done.11
  80.9 0.5 copy-done.9
  82.1 0.8 copy-done.3
  83.5 0.7 copy-done.16
  84.7 0.4 copy-done.17
  85.7 0.4 copy-done.19
  86.1 0.4 multiply_convert_fusion.1
  86.8 0.5 copy-done.6
  87.3 3.5 collective-permute-start.3
  90.9 3.2 collective-permute-start.2
  94.0 5.2 %collective-permute-start.10 = (bf16[1,64,256]{2,1,0:T(8,128)(2,1)S(1)}, bf16[1,64,256]{2,1,0:T(8,128)(2,1)S(1)}, u32[]{:S(2)}, u32[]{:S(2)}) collective-permute-start(bf16[1,64,256]{2,1,0:T(8,128)(2,1)S(1)} %slice.321), channel_id=1, source_target_pairs={{0,504},{8,0},{16,8},{24,16},{32,24},{40,32},{48,40},{56,48},{64,5... | collective-permute-start | bytes 98312 | tf_op jit(solution)/shard_map/ppermute | solution.py:12
  100.2 1.3 collective-permute-start.11
  101.8 6.7 %collective-permute-done.11 = bf16[9,1,256]{2,1,0:T(2,128)(2,1)S(1)} collective-permute-done((bf16[9,1,256]{2,1,0:T(2,128)(2,1)S(1)}, bf16[9,1,256]{2,1,0:T(2,128)(2,1)S(1)}, u32[]{:S(2)}, u32[]{:S(2)}) %collective-permute-start.11) | collective-permute-done | bytes 4640 | tf_op jit(solution)/shard_map/ppermute | solution.py:18
  109.7 1.9 collective-permute-start.5
  111.7 7.5 %collective-permute-start.4 = (bf16[16,4,256]{2,1,0:T(4,128)(2,1)S(1)}, bf16[16,4,256]{2,1,0:T(4,128)(2,1)S(1)}, u32[]{:S(2)}, u32[]{:S(2)}) collective-permute-start(bf16[16,4,256]{2,1,0:T(4,128)(2,1)S(1)} %get-tuple-element.25), channel_id=1, source_target_pairs={{0,4},{4,0},{1,5},{5,1},{2,6},{6,2},{3,7},{7,3},{8,12},{12,8},{9,1... | collective-permute-start | bytes 98312 | tf_op jit(solution)/shard_map/ppermute | solution.py:27
  119.2 1.1 copy.11
  120.3 1.2 convert_element_type.63
  121.6 0.4 maximum_select_fusion
  124.9 2.7 copy.13
  127.9 0.7 copy-done.5
  130.7 0.5 copy-done.7
  131.2 0.9 add_convert_fusion
  132.0 279.5 %all-reduce.3.cloned.1.call-done = f32[589824]{0:T(1024)} async-done(((f32[589824]{0:T(1024)}), f32[589824]{0:T(1024)}) %all-reduce.3.cloned.1.call-update) | async-done | bytes 2359312
  411.6 1.4 dynamic-slice
  (106 shorter events, 12.4 us)
Async XLA Ops:
  7.2 16.0 %copy-start.1 = (bf16[1,16,128,256]{3,2,1,0:T(8,128)(2,1)S(1)}, bf16[1,16,128,256]{3,2,1,0:T(8,128)(2,1)}, u32[]{:S(2)}) copy-start(bf16[1,16,128,256]{3,2,1,0:T(8,128)(2,1)} %param.4) | copy-start | bytes 3145732
  7.2 51.9 %all-gather.3.cloned.1.call-start = ((), (), s32[]{:S(2)}) async-start(), calls=%async_computation | async-start | bytes 1474560 | tf_op jit(solution)/shard_map/all_gather | solution.py:122
  7.9 69.0 %all-gather.5.cloned.1.call-start = ((), (), s32[]{:S(2)}) async-start(), calls=%async_computation.1 | async-start | bytes 1474560 | tf_op jit(solution)/shard_map/all_gather | solution.py:123
  9.6 32.2 %collective-permute-start.7 = (bf16[4,64,256]{2,1,0:T(8,128)(2,1)}, bf16[4,64,256]{2,1,0:T(8,128)(2,1)S(1)}, u32[]{:S(2)}, u32[]{:S(2)}) collective-permute-start(bf16[4,64,256]{2,1,0:T(8,128)(2,1)} %get-tuple-element.30), channel_id=1, source_target_pairs={{8,0},{16,8},{24,16},{32,24},{40,32},{48,40},{56,48},{64,56},{72,6... | collective-permute-start | bytes 393224 | tf_op jit(solution)/shard_map/ppermute | solution.py:30
  18.4 23.4 %collective-permute-start.6 = (bf16[4,64,256]{2,1,0:T(8,128)(2,1)S(1)}, bf16[4,64,256]{2,1,0:T(8,128)(2,1)S(1)}, u32[]{:S(2)}, u32[]{:S(2)}) collective-permute-start(bf16[4,64,256]{2,1,0:T(8,128)(2,1)S(1)} %get-tuple-element.29), channel_id=1, source_target_pairs={{0,8},{8,16},{16,24},{24,32},{32,40},{40,48},{48,56},{56,64},{64,7... | collective-permute-start | bytes 393224 | tf_op jit(solution)/shard_map/ppermute | solution.py:27
  20.3 391.2 %all-reduce.3.cloned.1.call-start = ((), (), s32[]{:S(2)}) async-start(), calls=%async_computation.2 | async-start | bytes 4718592
  21.2 12.7 %collective-permute-start = (bf16[1,128,256]{2,1,0:T(8,128)(2,1)S(1)}, bf16[1,128,256]{2,1,0:T(8,128)(2,1)S(1)}, u32[]{:S(2)}, u32[]{:S(2)}) collective-permute-start(bf16[1,128,256]{2,1,0:T(8,128)(2,1)S(1)} %slice_bitcast_fusion.53), channel_id=1, source_target_pairs={{0,8},{8,16},{16,24},{24,32},{32,40},{40,48},{48,56},{56,64},{64,7... | collective-permute-start | bytes 196616 | tf_op jit(solution)/shard_map/ppermute | solution.py:12
  34.1 7.7 %copy-start = (bf16[1,8,64,256]{3,2,1,0:T(8,128)(2,1)S(1)}, bf16[1,8,64,256]{3,2,1,0:T(8,128)(2,1)}, u32[]{:S(2)}) copy-start(bf16[1,8,64,256]{3,2,1,0:T(8,128)(2,1)} %param.7) | copy-start | bytes 786436
  34.9 16.1 %collective-permute-start.1 = (bf16[17,1,256]{2,1,0:T(2,128)(2,1)S(1)}, bf16[17,1,256]{2,1,0:T(2,128)(2,1)S(1)}, u32[]{:S(2)}, u32[]{:S(2)}) collective-permute-start(bf16[17,1,256]{2,1,0:T(2,128)(2,1)S(1)} %fusion.27), channel_id=1, source_target_pairs={{0,4},{1,5},{2,6},{3,7},{8,12},{9,13},{10,14},{11,15},{16,20},{17,... | collective-permute-start | bytes 26120 | tf_op jit(solution)/shard_map/ppermute | solution.py:18
  41.8 15.6 %collective-permute-start.9 = (bf16[16,4,256]{2,1,0:T(4,128)(2,1)S(1)}, bf16[16,4,256]{2,1,0:T(4,128)(2,1)S(1)}, u32[]{:S(2)}, u32[]{:S(2)}) collective-permute-start(bf16[16,4,256]{2,1,0:T(4,128)(2,1)S(1)} %get-tuple-element.24), channel_id=1, source_target_pairs={{4,0},{0,4},{5,1},{1,5},{6,2},{2,6},{7,3},{3,7},{12,8},{8,12},{13,... | collective-permute-start | bytes 98312 | tf_op jit(solution)/shard_map/ppermute | solution.py:30
  43.7 13.6 %collective-permute-start.8 = (bf16[16,4,256]{2,1,0:T(4,128)(2,1)S(1)}, bf16[16,4,256]{2,1,0:T(4,128)(2,1)S(1)}, u32[]{:S(2)}, u32[]{:S(2)}) collective-permute-start(bf16[16,4,256]{2,1,0:T(4,128)(2,1)S(1)} %get-tuple-element.23), channel_id=1, source_target_pairs={{0,4},{4,0},{1,5},{5,1},{2,6},{6,2},{3,7},{7,3},{8,12},{12,8},{9,1... | collective-permute-start | bytes 98312 | tf_op jit(solution)/shard_map/ppermute | solution.py:27
  76.9 2.5 copy-start.2
  76.9 2.5 copy-start.13
  78.1 1.5 copy-start.12
  79.4 1.0 copy-start.11
  79.7 1.0 copy-start.10
  80.4 1.0 copy-start.9
  80.6 1.0 copy-start.8
  81.6 1.3 copy-start.3
  81.6 1.3 copy-start.18
  83.2 1.0 copy-start.16
  83.5 1.0 copy-start.15
  84.1 1.0 copy-start.17
  84.4 1.0 copy-start.14
  85.1 1.0 copy-start.19
  86.5 0.8 copy-start.6
  87.3 22.4 %collective-permute-start.3 = (bf16[4,64,256]{2,1,0:T(8,128)(2,1)S(1)}, bf16[4,64,256]{2,1,0:T(8,128)(2,1)S(1)}, u32[]{:S(2)}, u32[]{:S(2)}) collective-permute-start(bf16[4,64,256]{2,1,0:T(8,128)(2,1)S(1)} %get-tuple-element.32), channel_id=1, source_target_pairs={{8,0},{16,8},{24,16},{32,24},{40,32},{48,40},{56,48},{64,56},{72,6... | collective-permute-start | bytes 393224 | tf_op jit(solution)/shard_map/ppermute | solution.py:30
  90.9 18.8 %collective-permute-start.2 = (bf16[4,64,256]{2,1,0:T(8,128)(2,1)S(1)}, bf16[4,64,256]{2,1,0:T(8,128)(2,1)S(1)}, u32[]{:S(2)}, u32[]{:S(2)}) collective-permute-start(bf16[4,64,256]{2,1,0:T(8,128)(2,1)S(1)} %get-tuple-element.31), channel_id=1, source_target_pairs={{0,8},{8,16},{16,24},{24,32},{32,40},{40,48},{48,56},{56,64},{64,7... | collective-permute-start | bytes 393224 | tf_op jit(solution)/shard_map/ppermute | solution.py:27
  94.0 6.1 %collective-permute-start.10 = (bf16[1,64,256]{2,1,0:T(8,128)(2,1)S(1)}, bf16[1,64,256]{2,1,0:T(8,128)(2,1)S(1)}, u32[]{:S(2)}, u32[]{:S(2)}) collective-permute-start(bf16[1,64,256]{2,1,0:T(8,128)(2,1)S(1)} %slice.321), channel_id=1, source_target_pairs={{0,504},{8,0},{16,8},{24,16},{32,24},{40,32},{48,40},{56,48},{64,5... | collective-permute-start | bytes 98312 | tf_op jit(solution)/shard_map/ppermute | solution.py:12
  100.2 8.3 %collective-permute-start.11 = (bf16[9,1,256]{2,1,0:T(2,128)(2,1)S(1)}, bf16[9,1,256]{2,1,0:T(2,128)(2,1)S(1)}, u32[]{:S(2)}, u32[]{:S(2)}) collective-permute-start(bf16[9,1,256]{2,1,0:T(2,128)(2,1)S(1)} %pad_maximum_fusion.10), channel_id=1, source_target_pairs={{4,0},{5,1},{6,2},{7,3},{12,8},{13,9},{14,10},{15,11},{20,16},{21,... | collective-permute-start | bytes 13832 | tf_op jit(solution)/shard_map/ppermute | solution.py:18
  109.7 11.8 %collective-permute-start.5 = (bf16[16,4,256]{2,1,0:T(4,128)(2,1)S(1)}, bf16[16,4,256]{2,1,0:T(4,128)(2,1)S(1)}, u32[]{:S(2)}, u32[]{:S(2)}) collective-permute-start(bf16[16,4,256]{2,1,0:T(4,128)(2,1)S(1)} %get-tuple-element.26), channel_id=1, source_target_pairs={{4,0},{0,4},{5,1},{1,5},{6,2},{2,6},{7,3},{3,7},{12,8},{8,12},{13,... | collective-permute-start | bytes 98312 | tf_op jit(solution)/shard_map/ppermute | solution.py:30
  111.7 9.9 %collective-permute-start.4 = (bf16[16,4,256]{2,1,0:T(4,128)(2,1)S(1)}, bf16[16,4,256]{2,1,0:T(4,128)(2,1)S(1)}, u32[]{:S(2)}, u32[]{:S(2)}) collective-permute-start(bf16[16,4,256]{2,1,0:T(4,128)(2,1)S(1)} %get-tuple-element.25), channel_id=1, source_target_pairs={{0,4},{4,0},{1,5},{5,1},{2,6},{6,2},{3,7},{7,3},{8,12},{12,8},{9,1... | collective-permute-start | bytes 98312 | tf_op jit(solution)/shard_map/ppermute | solution.py:27
  122.2 0.8 copy-start.4
  127.6 0.9 copy-start.5
  130.1 1.0 copy-start.7
Sparse Core Ops, SparseCore 0:
  10.1 34.2 all-gather.2
  46.5 30.3 all-gather.4
  127.7 283.7 all-reduce.2
where the time goes:
time: 420 us; the launch traced here: 419 us
  waiting for transfers between devices  302 us (72%)
  starting transfers between devices  51.3 us (12%)
  local copies, waits for them, and re-layouts  33 us (8%)
  matrix products  15.2 us (4%)
  between operations  14.5 us (3%)
    unnamed x4, waiting for transfers between devices  280 us
    ppermute x4, starting transfers between devices, padded(): lax.ppermute(lax.slice_in_dim(block, block.shape[dim] - width, None, axis...  19.8 us
    slice x12, local copies, waits for them, and re-layouts, tap_conv(): extended[row_at:row_at + stride * rows_out:stride, col_at:col_at + stride...  19.1 us
    ppermute x4, starting transfers between devices, padded(): lax.ppermute(lax.slice_in_dim(block, 0, width, axis=dim), axis, backward)  16.1 us
    all_gather x1, waiting for transfers between devices, body(): lax.all_gather(second_kernel, 'batch', axis=2, tiled=True)  15.4 us
    dot_general x36, matrix products, tap_conv(): jnp.dot(window, kernel, preferred_element_type=jnp.float32)  12.7 us
    unnamed x42, local copies, waits for them, and re-layouts  9.14 us
  transfers between devices with their start and end apart: 15, of which 3 were waited for; matrix products, arithmetic and copies ran while one was open for 8% of the time, Pallas kernels for 0%

commit v1 on v0

v1 whole, which is shorter than its diff:
```python
import jax
import jax.numpy as jnp
from jax import lax
from jax.experimental import pallas as pl
from jax.experimental.pallas import tpu as pltpu
from jax.sharding import PartitionSpec as P

BF = jnp.bfloat16
F32 = jnp.float32
SHIFTS = (4, 0, -4)


def dot_nt(a, b):
    return lax.dot_general(a, b, (((1,), (1,)), ((), ())), preferred_element_type=F32)


def dot_nn(a, b):
    return lax.dot_general(a, b, (((1,), (0,)), ((), ())), preferred_element_type=F32)


def kernel(
    snap_hbm, w1_hbm, w2_hbm, cot_hbm,
    enc_ref, ing_ref, kg_ref,
    snap, xs, colf, cols_s, cols_r, w1, w2, cotr, cot_sh, edgef, cedge_s, cedge_r, aedge_s, aedge_r,
    extf, cot_h, actr, act_pair, act_sh, pre, at, gbuf, xbuf, xr, ysum, ybuf, yr, zsum, pbuf, prec, fin,
    gp, gp1, gpf, gcol_s, gcol_r,
    loc_sem, wsend, wrecv, wfs, wfr, hs, hr, xss, xrs, yss, yrs, zss, zrs,
):
    a = lax.axis_index("azi")
    rad = lax.axis_index("rad")
    x = lax.axis_index("batch")
    core = lax.rem(a, 2)
    zlo = lax.rem(a // 2, 4)
    y = a // 8

    def dev(azi, r, b):
        return {"azi": azi, "rad": r, "batch": b}

    def signal(target):
        pl.semaphore_signal(barrier, inc=1, device_id=target, device_id_type=pl.DeviceIdType.MESH)

    def remote(src, dst, ss, rs, target):
        return pltpu.make_async_remote_copy(
            src_ref=src, dst_ref=dst, send_sem=ss, recv_sem=rs,
            device_id=target, device_id_type=pl.DeviceIdType.MESH,
        )

    other = dev(a + 1 - 2 * core, rad, x)
    up = dev(lax.rem(a + 63, 64), rad, x)
    down = dev(lax.rem(a + 1, 64), rad, x)
    band = dev(a, 1 - rad, x)
    x_peers = [dev(a, rad, lax.rem(x + d, 4)) for d in (1, 2, 3)]
    y_peers = [dev(lax.rem(y + d, 8) * 8 + zlo * 2 + core, rad, x) for d in range(1, 8)]
    own_home = zlo == x

    barrier = pltpu.get_barrier_semaphore()
    for target in [other, up, down, band] + x_peers + y_peers:
        signal(target)
    for cs in range(2):
        for zh in range(2):
            for zl in range(4):
                is_self = own_home & (core == cs) & (rad == zh) & (zlo == zl)

                @pl.when(jnp.logical_not(is_self))
                def _():
                    signal(dev((y * 4 + zl) * 2 + cs, zh, zlo))

    def shard_rows(w):
        return w.at[:, pl.ds(pl.multiple_of(64 * x, 64), 64), :]

    def half_rows(w, xi, k):
        return w.at[:, pl.ds(pl.multiple_of(64 * xi + 32 * k, 32), 32), :]

    lsnap = pltpu.make_async_copy(snap_hbm, snap.at[1:17], loc_sem.at[0])
    lw1 = pltpu.make_async_copy(w1_hbm, shard_rows(w1), loc_sem.at[1])
    lw2 = pltpu.make_async_copy(w2_hbm, shard_rows(w2), loc_sem.at[2])
    lcot = pltpu.make_async_copy(cot_hbm, cotr.at[4:12], loc_sem.at[3])
    for c in (lw1, lsnap, lcot, lw2):
        c.start()
    pl.semaphore_wait(barrier, jnp.where(own_home, 29, 30))

    def gather_send(w, w_hbm, base):
        out = []
        for d in range(3):
            src = w_hbm.at[:, pl.ds(pl.multiple_of(32 * core, 32), 32), :]
            c = remote(src, half_rows(w, x, core), wsend.at[base + d], wrecv.at[base + d], x_peers[d])
            c.start()
            out.append(c)
        return out

    def gather_forward(w, sends, base):
        out = []
        for d in range(3):
            sends[d].wait_recv()
            xi = lax.rem(x + 3 - d, 4)
            part = half_rows(w, xi, core)
            c = remote(part, part, wfs.at[base + d], wfr.at[base + d], other)
            c.start()
            out.append(c)
        return out

    g1 = gather_send(w1, w1_hbm, 0)
    hsnap = remote(snap_hbm.at[15], snap.at[0], hs.at[0], hr.at[0], down)
    hsnap.start()
    hcot_d = remote(cot_hbm.at[4:8], cotr.at[0:4], hs.at[1], hr.at[1], down)
    hcot_d.start()
    hcot_u = remote(cot_hbm.at[0:4], cotr.at[12:16], hs.at[2], hr.at[2], up)
    hcot_u.start()

    row_i = lax.broadcasted_iota(jnp.int32, (192, 128), 0)
    col_i = lax.broadcasted_iota(jnp.int32, (192, 128), 1)
    pick = jnp.where(col_i == 2 * lax.rem(row_i, 64) + row_i // 64 - 1, 1.0, 0.0).astype(BF)

    def split_row(e):
        got = dot_nn(pick, snap[e])
        for n in range(3):
            xs[n, e % 2, e // 2] = got[64 * n : 64 * n + 64].astype(BF)
        colf[e : e + 1, :] = got[191:192]

    colf[...] = jnp.zeros_like(colf)
    lsnap.wait()
    for e in range(1, 17):
        split_row(e)
    hsnap.wait()
    split_row(0)
    cols_s[...] = colf[...].astype(BF)
    hcols = remote(cols_s, cols_r, hs.at[3], hr.at[3], band)
    hcols.start()

    def edges(field, out):
        for r in range(16):
            low = field[r, 0:16, :].astype(F32)[0:4]
            high = field[r, 48:64, :].astype(F32)[12:16]
            edgef[4 * r : 4 * r + 4, :] = jnp.where(rad == 0, high, low)
        out[...] = edgef[...].astype(BF)

    def shifted(field, edge, sh):
        got = edge[...].astype(F32)
        for r in range(16):
            extf[r, 8:72, :] = field[r].astype(F32)
            part = got[4 * r : 4 * r + 4]
            extf[r, 4:8, :] = jnp.where(rad == 1, part, 0.0)
            extf[r, 72:76, :] = jnp.where(rad == 0, part, 0.0)
            sh[1, r] = field[r]
            sh[2, r] = extf[r, 4:68, :].astype(BF)
            sh[0, r] = extf[r, 12:76, :].astype(BF)

    lcot.wait()
    hcot_d.wait()
    hcot_u.wait()
    edges(cotr, cedge_s)
    hcedge = remote(cedge_s, cedge_r, hs.at[4], hr.at[4], band)
    hcedge.start()

    hcols.wait()
    in_row = lax.broadcasted_iota(jnp.int32, (16, 256), 0)
    colv = jnp.where(rad == 1, cols_r[...].astype(F32), 0.0)
    for e in range(17):
        tile = xs[0, e % 2, e // 2, 0:16, :].astype(F32)
        xs[0, e % 2, e // 2, 0:16, :] = jnp.where(in_row == 0, colv[e : e + 1], tile).astype(BF)

    f1 = gather_forward(w1, g1, 0)
    lw1.wait()

    hcedge.wait()
    shifted(cotr, cedge_r, cot_sh)
    mine = pl.ds(pl.multiple_of(128 * core, 128), 128)
    theirs = pl.ds(pl.multiple_of(128 * (1 - core), 128), 128)
    lhalf = pltpu.make_async_copy(cot_sh.at[:, :, :, mine], cot_h.at[core], loc_sem.at[4])
    lhalf.start()
    hhalf = remote(cot_sh.at[:, :, :, theirs], cot_h.at[core], hs.at[5], hr.at[5], other)
    hhalf.start()

    for d in range(3):
        f1[d].wait()
    for d in range(3):
        g1[d].wait_send()
    g2 = gather_send(w2, w2_hbm, 3)

    def conv1(b, _):
        at_row = 4 * b
        total = jnp.zeros((256, 256), F32)
        for t in range(9):
            m, n = t // 3, t % 3
            win = xs[n, m % 2, pl.ds(at_row + m // 2, 4)].reshape(256, 256)
            total = total + dot_nt(win, w1[t])
        pre[pl.ds(pl.multiple_of(256 * b, 256), 256), :] = total
        sig = 1.0 / (1.0 + jnp.exp(-total))
        act = (total * sig).astype(BF)
        actr[pl.ds(4 + at_row, 4)] = act.reshape(4, 64, 256)
        act_pair[core, pl.ds(pl.multiple_of(256 * b, 256), 256), :] = act
        return 0

    lax.fori_loop(0, 2, conv1, 0)
    hact = remote(act_pair.at[core], act_pair.at[core], hs.at[6], hr.at[6], other)
    hact.start()
    hact_d = remote(actr.at[8:12], actr.at[0:4], hs.at[7], hr.at[7], down)
    hact_d.start()
    hact_u = remote(actr.at[4:8], actr.at[12:16], hs.at[8], hr.at[8], up)
    hact_u.start()
    lhalf.wait()
    hhalf.wait()
    hact.wait()
    for k in range(2):
        at[:, 512 * k : 512 * k + 512] = act_pair[k].T

    def window(k, t):
        m, n = t // 3, t % 3
        return cot_h[k, n, 8 - 4 * m : 16 - 4 * m].reshape(512, 128)

    def put(t, value):
        first = 256 * t
        for q in range(32):
            lo, hi = max(72 * q, first), min(72 * q + 72, first + 256)
            if lo < hi:
                gbuf[q % 4, q // 4, lo - 72 * q : hi - 72 * q, :] = value[lo - first : hi - first] * (1.0 / 512.0)

    for t in range(0, 8, 2):
        total = jnp.zeros((256, 256), F32)
        for k in range(2):
            both = jnp.concatenate([window(k, t), window(k, t + 1)], axis=1)
            total = total + dot_nn(at[:, 512 * k : 512 * k + 512], both)
        put(t, total[:, 0:128])
        put(t + 1, total[:, 128:256])
    total = jnp.zeros((256, 128), F32)
    for k in range(2):
        total = total + dot_nn(at[:, 512 * k : 512 * k + 512], window(k, 8))
    put(8, total)
    for i in range(4):
        for j in range(8):
            gbuf[i, j, 72:80, :] = jnp.zeros((8, 128), F32)
    for i in range(4):
        xbuf[i] = gbuf[i].astype(BF)
    xc = []
    for d in range(3):
        c = remote(xbuf.at[lax.rem(x + 1 + d, 4)], xr.at[d], xss.at[d], xrs.at[d], x_peers[d])
        c.start()
        xc.append(c)

    hact_d.wait()
    hact_u.wait()
    edges(actr, aedge_s)
    haedge = remote(aedge_s, aedge_r, hs.at[9], hr.at[9], band)
    haedge.start()
    f2 = gather_forward(w2, g2, 3)
    lw2.wait()
    haedge.wait()
    shifted(actr, aedge_r, act_sh)

    for d in range(3):
        xc[d].wait()
    for j in range(8):
        s = gbuf[x, j]
        for d in range(3):
            s = s + xr[d, j].astype(F32)
        ysum[j] = s
        ybuf[j] = s.astype(BF)
    yc = []
    for d in range(7):
        c = remote(ybuf.at[lax.rem(y + 1 + d, 8)], yr.at[d], yss.at[d], yrs.at[d], y_peers[d])
        c.start()
        yc.append(c)

    for d in range(3):
        f2[d].wait()
    for d in range(3):
        g2[d].wait_send()

    def back(b, _):
        at_row = 4 * b
        cells = pl.ds(pl.multiple_of(256 * b, 256), 256)
        total = cot_sh[1, pl.ds(4 + at_row, 4)].reshape(256, 256).astype(F32)
        for t in range(9):
            m, n = t // 3, t % 3
            win = cot_sh[n, pl.ds(at_row + 8 - 4 * m, 4)].reshape(256, 256)
            total = total + dot_nn(win, w2[t])
        v = pre[cells, :]
        s = 1.0 / (1.0 + jnp.exp(-v))
        g = (total * (s * (1.0 + v * (1.0 - s)))).astype(BF)
        gp[pl.ds(at_row, 4)] = g.reshape(4, 64, 256)
        return 0

    lax.fori_loop(0, 2, back, 0)
    hgp = remote(gp.at[0], gp.at[8], hs.at[10], hr.at[10], up)
    hgp.start()

    for d in range(7):
        yc[d].wait()
    s = ysum[y]
    for d in range(7):
        s = s + yr[d].astype(F32)
    zsum[...] = s
    for p in range(16):
        pbuf[p] = zsum[(9 * p) // 2 : (9 * p) // 2 + 8, :]
    slot = core * 8 + rad * 4 + zlo
    zc = []
    for p in range(16):
        c1, zh, xp = p // 8, (p // 4) % 2, p % 4
        is_self = own_home & (core == c1) & (rad == zh) & (x == xp)
        rc = remote(pbuf.at[p], prec.at[slot], zss.at[p], zrs.at[slot], dev((y * 4 + x) * 2 + c1, zh, xp))
        lc = pltpu.make_async_copy(pbuf.at[p], prec.at[slot], zrs.at[slot])

        @pl.when(is_self)
        def _():
            lc.start()

        @pl.when(jnp.logical_not(is_self))
        def _():
            rc.start()

        zc.append((is_self, rc))

    def ahead(b, _):
        at_row = 4 * b
        total = act_sh[1, pl.ds(4 + at_row, 4)].reshape(256, 256).astype(F32)
        for t in range(9):
            m, n = t // 3, t % 3
            win = act_sh[2 - n, pl.ds(at_row + 4 * m, 4)].reshape(256, 256)
            total = total + dot_nt(win, w2[t])
        enc_ref[pl.ds(at_row, 4)] = total.astype(BF).reshape(4, 64, 256)
        return 0

    hgp.wait()
    for r in range(9):
        gpf[r, 0:64, :] = gp[r].astype(F32)
        colf[r : r + 1, :] = gpf[r, 0:1, :]
    gcol_s[...] = colf[0:16, :].astype(BF)
    hgcol = remote(gcol_s, gcol_r, hs.at[11], hr.at[11], band)
    hgcol.start()
    lax.fori_loop(0, 2, ahead, 0)
    hgcol.wait()
    colv = jnp.where(rad == 0, gcol_r[...].astype(F32), 0.0)
    for r in range(9):
        gpf[r, 64:65, :] = colv[r : r + 1]
        gp1[r] = gpf[r, 1:65, :].astype(BF)

    row_q = lax.broadcasted_iota(jnp.int32, (128, 128), 0)
    col_q = lax.broadcasted_iota(jnp.int32, (128, 128), 1)
    weave = jnp.where(col_q == lax.rem(row_q, 2) * 64 + row_q // 2, 1.0, 0.0).astype(BF)
    ptaps = (((1, 0),), ((2, 0), (0, 1)))

    def inward(b, _):
        at_row = 4 * b
        for rp in range(2):
            halves = []
            for cp in range(2):
                total = jnp.zeros((256, 256), F32)
                for m, rs in ptaps[rp]:
                    for n, cs in ptaps[cp]:
                        field = gp1 if cs else gp
                        win = field[pl.ds(at_row + rs, 4)].reshape(256, 256)
                        total = total + dot_nn(win, w1[3 * m + n])
                halves.append(total.astype(BF).reshape(4, 64, 256))
            for i in range(4):
                pair = jnp.concatenate([halves[0][i], halves[1][i]], axis=0)
                ing_ref[2 * (at_row + i) + rp] = dot_nn(weave, pair).astype(BF)
        return 0

    lax.fori_loop(0, 2, inward, 0)

    for s in range(16):
        pltpu.make_async_copy(pbuf.at[0], prec.at[s], zrs.at[s]).wait()
    for k in range(2):
        s = prec[8 * k]
        for i in range(1, 8):
            s = s + prec[8 * k + i]
        for i in range(5):
            fin[2 * i + k : 2 * i + k + 1, :] = s[i : i + 1]
    kg_ref[...] = jnp.where(lax.rem(x, 2) == 0, fin[0:9, :], fin[1:10, :])
    for is_self, rc in zc:
        @pl.when(jnp.logical_not(is_self))
        def _():
            rc.wait_send()


def body(snapshots, first_kernel, second_kernel, cotangent):
    def vm(shape, kind=BF):
        return pltpu.VMEM(shape, kind)

    dma = pltpu.SemaphoreType.DMA
    scratch = [
        vm((17, 128, 256)), vm((3, 2, 9, 64, 256)), vm((32, 256), F32), vm((32, 256)), vm((32, 256)),
        vm((9, 256, 256)), vm((9, 256, 256)), vm((16, 64, 256)), vm((3, 16, 64, 256)),
        vm((64, 256), F32), vm((64, 256)), vm((64, 256)), vm((64, 256)), vm((64, 256)),
        vm((16, 80, 256), F32), vm((2, 3, 16, 64, 128)), vm((16, 64, 256)), vm((2, 512, 256)),
        vm((3, 16, 64, 256)), vm((512, 256), F32), vm((256, 1024)),
        vm((4, 8, 80, 128), F32), vm((4, 8, 80, 128)), vm((3, 8, 80, 128)),
        vm((8, 80, 128), F32), vm((8, 80, 128)), vm((7, 80, 128)),
        vm((80, 128), F32), vm((16, 8, 128), F32), vm((16, 8, 128), F32), vm((16, 128), F32),
        vm((9, 64, 256)), vm((9, 64, 256)), vm((9, 80, 256), F32), vm((16, 256)), vm((16, 256)),
        dma((5,)), dma((6,)), dma((6,)), dma((6,)), dma((6,)), dma((12,)), dma((12,)),
        dma((3,)), dma((3,)), dma((7,)), dma((7,)), dma((16,)), dma((16,)),
    ]
    enc, ing, kg = pl.pallas_call(
        kernel,
        name="section",
        out_shape=(
            jax.ShapeDtypeStruct((8, 64, 256), BF),
            jax.ShapeDtypeStruct((16, 128, 256), BF),
            jax.ShapeDtypeStruct((9, 128), F32),
        ),
        in_specs=[pl.BlockSpec(memory_space=pl.ANY)] * 4,
        out_specs=[pl.BlockSpec(memory_space=pltpu.VMEM)] * 3,
        scratch_shapes=scratch,
        compiler_params=pltpu.CompilerParams(
            collective_id=0, has_side_effects=True, vmem_limit_bytes=56 << 20
        ),
    )(
        snapshots[0],
        jnp.swapaxes(first_kernel, 1, 2),
        jnp.swapaxes(second_kernel, 1, 2),
        cotangent[0],
    )
    return enc[None], ing[None], kg.reshape(1152)


def solution(mesh):
    return jax.shard_map(
        body,
        mesh=mesh,
        in_specs=(
            P("batch", "azi", "rad", None),
            P(None, None, "batch"),
            P(None, None, "batch"),
            P("batch", "azi", "rad", None),
        ),
        out_specs=(
            P("batch", "azi", "rad", None),
            P("batch", "azi", "rad", None),
            P(("azi", "rad", "batch")),
        ),
        check_vma=False,
    )
```

time: 420 us -> 64.5 us (0.15)
  waiting for transfers between devices: 302 us -> 0 us
  Pallas kernels: 0 us -> 59.1 us
  starting transfers between devices: 51.3 us -> 0 us
  local copies, waits for them, and re-layouts: 33 us -> 4.57 us
  matrix products: 15.2 us -> 0 us
  between operations: 14.5 us -> 0.64 us
    unnamed x4 -> x0, waiting for transfers between devices: 280 us -> none
    pallas_call x0 -> x1, Pallas kernels: none -> 59.1 us  [body(): pl.pallas_call(kernel, name='section', out_shape=(jax.ShapeDtypeStruct((8...]
    ppermute x12 -> x0, starting transfers between devices: 51.2 us -> none  [the longest x4 19.8 us: padded(): lax.ppermute(lax.slice_in_dim(block, block.shape[dim] - width, None, axis...]
    slice x16 -> x0, local copies, waits for them, and re-layouts: 21.6 us -> none  [the longest x12 19.1 us: tap_conv(): extended[row_at:row_at + stride * rows_out:stride, col_at:col_at + stride...]
    all_gather x2 -> x0, waiting for transfers between devices: 15.4 us -> none  [the longest x1 15.4 us: body(): lax.all_gather(second_kernel, 'batch', axis=2, tiled=True)]
    dot_general x45 -> x0, matrix products: 15.2 us -> none  [the longest x36 12.7 us: tap_conv(): jnp.dot(window, kernel, preferred_element_type=jnp.float32)]
    ppermute x12 -> x0, waiting for transfers between devices: 6.77 us -> none  [the longest x2 6.75 us: passed_along(): return lax.ppermute(x, axis, pairs)]
    unnamed x42 -> x5, local copies, waits for them, and re-layouts: 9.14 us -> 4.57 us
  transfers between devices with their start and end apart: 15 -> 0, of which waited for: 3 -> 0; matrix products, arithmetic and copies ran while one was open for 8% -> 0% of each run, Pallas kernels for 0% -> 0%
where the time goes in v1:
time: 64.5 us; the launch traced here: 64.3 us
  Pallas kernels  59.1 us (92%)
  local copies, waits for them, and re-layouts  4.57 us (7%)
    pallas_call x1, Pallas kernels, body(): pl.pallas_call(kernel, name='section', out_shape=(jax.ShapeDtypeStruct((8...  59.1 us
    unnamed x5, local copies, waits for them, and re-layouts  4.57 us

profile of v1, /device:TPU:1, one launch (start us, length us, event | category | flops | bytes accessed | tf_op | source)
XLA Modules:
  0.0 64.3 jit_solution(12548041882683333094)
XLA Ops:
  0.6 59.1 %section.1 = (bf16[8,64,256]{2,1,0:T(8,128)(2,1)}, bf16[16,128,256]{2,1,0:T(8,128)(2,1)}, f32[9,128]{1,0:T(8,128)}) custom-call(bf16[16,128,256]{2,1,0:T(8,128)(2,1)} %bitcast.7, bf16[9,64,256]{2,1,0:T(8,128)(2,1)} %bitcast.9, bf16[9,64,256]{2,1,0:T(8,128)(2,1)} %bitcast.10, bf16[8,64,256]{2,1,0:T(8,128)(2,1)} %bitcast.12), custom_call_target="tpu_custom_call" | custom-call | tf_op jit(solution)/shard_map/section/pallas_call | solution.py:394
  59.7 1.7 %copy.10 = bf16[1,8,64,256]{3,2,1,0:T(8,128)(2,1)} copy(bf16[1,8,64,256]{3,2,1,0:T(8,128)(2,1)} %bitcast.11) | data formatting | bytes 524288
  61.4 0.0 copy-start
  61.4 2.3 %copy.11 = bf16[1,16,128,256]{3,2,1,0:T(8,128)(2,1)} copy(bf16[1,16,128,256]{3,2,1,0:T(8,128)(2,1)} %bitcast.8) | data formatting | bytes 2097152
  63.7 0.0 copy-done
  63.7 0.6 copy.12
Async XLA Ops:
  61.4 2.3 %copy-start = (f32[9,128]{1,0:T(8,128)S(1)}, f32[9,128]{1,0:T(8,128)}, u32[]{:S(2)}) copy-start(f32[9,128]{1,0:T(8,128)} %get-tuple-element.8) | copy-start | bytes 13828

commit v2 on v1

--- a/solution.py
+++ b/solution.py
@@ -21,9 +21,9 @@
 def kernel(
     snap_hbm, w1_hbm, w2_hbm, cot_hbm,
     enc_ref, ing_ref, kg_ref,
-    snap, xs, colf, cols_s, cols_r, w1, w2, cotr, cot_sh, edgef, cedge_s, cedge_r, aedge_s, aedge_r,
-    extf, cot_h, actr, act_pair, act_sh, pre, at, gbuf, xbuf, xr, ysum, ybuf, yr, zsum, pbuf, prec, fin,
-    gp, gp1, gpf, gcol_s, gcol_r,
+    snap, xs, colf, cols_s, cols_r, cols_c, w1, w2, cot24, cot_sh, cot_h, edgef, cedge_s, cedge_r, aedge_s, aedge_r,
+    extf, actr, act_pair, act_sh, pre, at, g1, g2, xbuf1, xr1, s1, ybuf1, yr1, ybuf2, yr2, s2, xbuf2, xr2,
+    zsum, pbuf, prec, fin, gp, gp1, gpf, gcol_s, gcol_r,
     loc_sem, wsend, wrecv, wfs, wfr, hs, hr, xss, xrs, yss, yrs, zss, zrs,
 ):
     a = lax.axis_index("azi")
@@ -49,12 +49,20 @@
     up = dev(lax.rem(a + 63, 64), rad, x)
     down = dev(lax.rem(a + 1, 64), rad, x)
     band = dev(a, 1 - rad, x)
+    step = 2 * core - 1
+    near = dev(lax.rem(a + 64 + step, 64), rad, x)
+    far = dev(lax.rem(a + 64 + 2 * step, 64), rad, x)
+    far_from = dev(lax.rem(a + 64 - 2 * step, 64), rad, x)
+
+    def across(target):
+        return dev(target["azi"], 1 - rad, x)
+
     x_peers = [dev(a, rad, lax.rem(x + d, 4)) for d in (1, 2, 3)]
     y_peers = [dev(lax.rem(y + d, 8) * 8 + zlo * 2 + core, rad, x) for d in range(1, 8)]
     own_home = zlo == x
 
     barrier = pltpu.get_barrier_semaphore()
-    for target in [other, up, down, band] + x_peers + y_peers:
+    for target in [other, up, down, band, far_from, across(other), across(near), across(far_from), across(up)] + x_peers + y_peers:
         signal(target)
     for cs in range(2):
         for zh in range(2):
@@ -74,23 +82,34 @@
     lsnap = pltpu.make_async_copy(snap_hbm, snap.at[1:17], loc_sem.at[0])
     lw1 = pltpu.make_async_copy(w1_hbm, shard_rows(w1), loc_sem.at[1])
     lw2 = pltpu.make_async_copy(w2_hbm, shard_rows(w2), loc_sem.at[2])
-    lcot = pltpu.make_async_copy(cot_hbm, cotr.at[4:12], loc_sem.at[3])
-    for c in (lw1, lsnap, lcot, lw2):
-        c.start()
-    pl.semaphore_wait(barrier, jnp.where(own_home, 29, 30))
+    own_rows = pl.ds(4 + 8 * core, 8)
+    lcot = pltpu.make_async_copy(cot_hbm, cot24.at[own_rows], loc_sem.at[3])
+    for c in (lcot, lsnap, lw1, lw2):
+        c.start()
+
+    def edge(tile_of, out, r):
+        low = tile_of(0).astype(F32)[0:4]
+        high = tile_of(48).astype(F32)[12:16]
+        out[4 * r : 4 * r + 4, :] = jnp.where(rad == 0, high, low)
+
+    lcot.wait()
+    for r in range(8):
+        edge(lambda c: cot24[4 + 8 * core + r, c : c + 16, :], edgef, r)
+    cedge_s[...] = edgef[0:32, :].astype(BF)
+    pl.semaphore_wait(barrier, jnp.where(own_home, 34, 35))
 
     def gather_send(w, w_hbm, base):
         out = []
-        for d in range(3):
+        for d in (1, 0, 2):
             src = w_hbm.at[:, pl.ds(pl.multiple_of(32 * core, 32), 32), :]
             c = remote(src, half_rows(w, x, core), wsend.at[base + d], wrecv.at[base + d], x_peers[d])
             c.start()
             out.append(c)
-        return out
+        return [out[1], out[0], out[2]]
 
     def gather_forward(w, sends, base):
         out = []
-        for d in range(3):
+        for d in (0, 2, 1):
             sends[d].wait_recv()
             xi = lax.rem(x + 3 - d, 4)
             part = half_rows(w, xi, core)
@@ -99,13 +118,26 @@
             out.append(c)
         return out
 
-    g1 = gather_send(w1, w1_hbm, 0)
+    g1s = gather_send(w1, w1_hbm, 0)
     hsnap = remote(snap_hbm.at[15], snap.at[0], hs.at[0], hr.at[0], down)
     hsnap.start()
-    hcot_d = remote(cot_hbm.at[4:8], cotr.at[0:4], hs.at[1], hr.at[1], down)
-    hcot_d.start()
-    hcot_u = remote(cot_hbm.at[0:4], cotr.at[12:16], hs.at[2], hr.at[2], up)
-    hcot_u.start()
+    edge_rows = pl.ds(4 * core, 4)
+    far_rows = pl.ds(20 * (1 - core), 4)
+    half = pl.ds(pl.multiple_of(128 * core, 128), 128)
+    cot_halo = [
+        remote(cot_hbm.at[edge_rows], cot24.at[far_rows], hs.at[1], hr.at[1], near),
+        remote(cot_hbm.at[edge_rows, :, half], cot24.at[far_rows, :, half], hs.at[2], hr.at[2], far),
+        remote(cot_hbm, cot24.at[own_rows], hs.at[4], hr.at[4], other),
+    ]
+    mid = pl.ds(pl.multiple_of(16 + 32 * core, 16), 32)
+    tip = pl.ds(pl.multiple_of(80 * (1 - core), 16), 16)
+    tip_s = pl.ds(pl.multiple_of(16 * core, 16), 16)
+    for i, target in ((12, band), (13, across(other))):
+        cot_halo.append(remote(cedge_s, cedge_r.at[mid], hs.at[i], hr.at[i], target))
+    for i, target in ((14, across(near)), (15, across(far))):
+        cot_halo.append(remote(cedge_s.at[tip_s], cedge_r.at[tip], hs.at[i], hr.at[i], target))
+    for c in cot_halo:
+        c.start()
 
     row_i = lax.broadcasted_iota(jnp.int32, (192, 128), 0)
     col_i = lax.broadcasted_iota(jnp.int32, (192, 128), 1)
@@ -117,25 +149,54 @@
             xs[n, e % 2, e // 2] = got[64 * n : 64 * n + 64].astype(BF)
         colf[e : e + 1, :] = got[191:192]
 
-    colf[...] = jnp.zeros_like(colf)
     lsnap.wait()
     for e in range(1, 17):
         split_row(e)
+    cols_s[...] = colf[1:17, :].astype(BF)
+    hcols = remote(cols_s, cols_r, hs.at[3], hr.at[3], band)
+    hcols.start()
+    hcorner = remote(cols_s, cols_c, hs.at[5], hr.at[5], across(down))
+    hcorner.start()
+
+    for c in cot_halo:
+        c.wait()
+    got = cedge_r[...].astype(F32)
+    for r in range(24):
+        extf[r, 8:72, :] = cot24[r].astype(F32)
+        part = got[4 * r : 4 * r + 4]
+        extf[r, 4:8, :] = jnp.where(rad == 1, part, 0.0)
+        extf[r, 72:76, :] = jnp.where(rad == 0, part, 0.0)
+        for n, start in ((0, 12), (1, 8), (2, 4)):
+            value = extf[r, start : start + 64, :].astype(BF)
+            cot_sh[n, r] = value
+            cot_h[n, r] = jnp.where(core == 0, value[:, 0:128], value[:, 128:256])
+
+    f1 = gather_forward(w1, g1s, 0)
+    g2s = gather_send(w2, w2_hbm, 3)
+
     hsnap.wait()
     split_row(0)
-    cols_s[...] = colf[...].astype(BF)
-    hcols = remote(cols_s, cols_r, hs.at[3], hr.at[3], band)
-    hcols.start()
+    hcols.wait()
+    hcorner.wait()
+    in_row = lax.broadcasted_iota(jnp.int32, (16, 256), 0)
+    colv = jnp.where(rad == 1, cols_r[...].astype(F32), 0.0)
+    corner = jnp.where(rad == 1, cols_c[...].astype(F32), 0.0)
+    for e in range(17):
+        tile = xs[0, e % 2, e // 2, 0:16, :].astype(F32)
+        side = colv[e - 1 : e] if e else corner[15:16]
+        xs[0, e % 2, e // 2, 0:16, :] = jnp.where(in_row == 0, side, tile).astype(BF)
+    lw1.wait()
+    for d in range(3):
+        f1[d].wait()
+        g1s[d].wait_send()
 
     def edges(field, out):
         for r in range(16):
-            low = field[r, 0:16, :].astype(F32)[0:4]
-            high = field[r, 48:64, :].astype(F32)[12:16]
-            edgef[4 * r : 4 * r + 4, :] = jnp.where(rad == 0, high, low)
+            edge(lambda c: field[r, c : c + 16, :], edgef, r)
         out[...] = edgef[...].astype(BF)
 
-    def shifted(field, edge, sh):
-        got = edge[...].astype(F32)
+    def shifted(field, edge_got, sh):
+        got = edge_got[...].astype(F32)
         for r in range(16):
             extf[r, 8:72, :] = field[r].astype(F32)
             part = got[4 * r : 4 * r + 4]
@@ -144,38 +205,6 @@
             sh[1, r] = field[r]
             sh[2, r] = extf[r, 4:68, :].astype(BF)
             sh[0, r] = extf[r, 12:76, :].astype(BF)
-
-    lcot.wait()
-    hcot_d.wait()
-    hcot_u.wait()
-    edges(cotr, cedge_s)
-    hcedge = remote(cedge_s, cedge_r, hs.at[4], hr.at[4], band)
-    hcedge.start()
-
-    hcols.wait()
-    in_row = lax.broadcasted_iota(jnp.int32, (16, 256), 0)
-    colv = jnp.where(rad == 1, cols_r[...].astype(F32), 0.0)
-    for e in range(17):
-        tile = xs[0, e % 2, e // 2, 0:16, :].astype(F32)
-        xs[0, e % 2, e // 2, 0:16, :] = jnp.where(in_row == 0, colv[e : e + 1], tile).astype(BF)
-
-    f1 = gather_forward(w1, g1, 0)
-    lw1.wait()
-
-    hcedge.wait()
-    shifted(cotr, cedge_r, cot_sh)
-    mine = pl.ds(pl.multiple_of(128 * core, 128), 128)
-    theirs = pl.ds(pl.multiple_of(128 * (1 - core), 128), 128)
-    lhalf = pltpu.make_async_copy(cot_sh.at[:, :, :, mine], cot_h.at[core], loc_sem.at[4])
-    lhalf.start()
-    hhalf = remote(cot_sh.at[:, :, :, theirs], cot_h.at[core], hs.at[5], hr.at[5], other)
-    hhalf.start()
-
-    for d in range(3):
-        f1[d].wait()
-    for d in range(3):
-        g1[d].wait_send()
-    g2 = gather_send(w2, w2_hbm, 3)
 
     def conv1(b, _):
         at_row = 4 * b
@@ -198,81 +227,99 @@
     hact_d.start()
     hact_u = remote(actr.at[4:8], actr.at[12:16], hs.at[8], hr.at[8], up)
     hact_u.start()
-    lhalf.wait()
-    hhalf.wait()
     hact.wait()
     for k in range(2):
         at[:, 512 * k : 512 * k + 512] = act_pair[k].T
 
-    def window(k, t):
+    def window(t):
         m, n = t // 3, t % 3
-        return cot_h[k, n, 8 - 4 * m : 16 - 4 * m].reshape(512, 128)
+        return cot_h[n, 8 - 4 * m : 24 - 4 * m].reshape(1024, 128)
 
     def put(t, value):
         first = 256 * t
+        value = value * (1.0 / 512.0)
         for q in range(32):
-            lo, hi = max(72 * q, first), min(72 * q + 72, first + 256)
-            if lo < hi:
-                gbuf[q % 4, q // 4, lo - 72 * q : hi - 72 * q, :] = value[lo - first : hi - first] * (1.0 / 512.0)
+            for lo, hi in ((72 * q, 72 * q + 56), (72 * q + 56, 72 * q + 72)):
+                part = hi - lo
+                a0, a1 = max(lo, first), min(hi, first + 256)
+                if a0 >= a1:
+                    continue
+                rows = value[a0 - first : a1 - first]
+                if part == 56:
+                    g1[q % 4, 56 * (q // 4) + a0 - lo : 56 * (q // 4) + a1 - lo, :] = rows
+                else:
+                    g2[q // 4, 16 * (q % 4) + a0 - lo : 16 * (q % 4) + a1 - lo, :] = rows
 
     for t in range(0, 8, 2):
-        total = jnp.zeros((256, 256), F32)
-        for k in range(2):
-            both = jnp.concatenate([window(k, t), window(k, t + 1)], axis=1)
-            total = total + dot_nn(at[:, 512 * k : 512 * k + 512], both)
+        both = jnp.concatenate([window(t), window(t + 1)], axis=1)
+        total = dot_nn(at[...], both)
         put(t, total[:, 0:128])
         put(t + 1, total[:, 128:256])
-    total = jnp.zeros((256, 128), F32)
-    for k in range(2):
-        total = total + dot_nn(at[:, 512 * k : 512 * k + 512], window(k, 8))
-    put(8, total)
+    put(8, dot_nn(at[...], window(8)))
     for i in range(4):
-        for j in range(8):
-            gbuf[i, j, 72:80, :] = jnp.zeros((8, 128), F32)
-    for i in range(4):
-        xbuf[i] = gbuf[i].astype(BF)
-    xc = []
-    for d in range(3):
-        c = remote(xbuf.at[lax.rem(x + 1 + d, 4)], xr.at[d], xss.at[d], xrs.at[d], x_peers[d])
-        c.start()
-        xc.append(c)
+        xbuf1[i] = g1[i].astype(BF)
+    xc1 = []
+    for d in (1, 0, 2):
+        c = remote(xbuf1.at[lax.rem(x + 1 + d, 4)], xr1.at[d], xss.at[d], xrs.at[d], x_peers[d])
+        c.start()
+        xc1.append(c)
+    for i in range(8):
+        ybuf2[i] = g2[i].astype(BF)
+    yc2 = []
+    for d in (3, 2, 4, 1, 5, 0, 6):
+        c = remote(ybuf2.at[lax.rem(y + 1 + d, 8)], yr2.at[d], yss.at[d], yrs.at[d], y_peers[d])
+        c.start()
+        yc2.append(c)
 
     hact_d.wait()
     hact_u.wait()
     edges(actr, aedge_s)
     haedge = remote(aedge_s, aedge_r, hs.at[9], hr.at[9], band)
     haedge.start()
-    f2 = gather_forward(w2, g2, 3)
+    f2 = gather_forward(w2, g2s, 3)
     lw2.wait()
-    haedge.wait()
-    shifted(actr, aedge_r, act_sh)
-
-    for d in range(3):
-        xc[d].wait()
+
+    for c in xc1:
+        c.wait()
     for j in range(8):
-        s = gbuf[x, j]
+        rows = slice(56 * j, 56 * j + 56)
+        s = g1[x, rows, :]
         for d in range(3):
-            s = s + xr[d, j].astype(F32)
-        ysum[j] = s
-        ybuf[j] = s.astype(BF)
-    yc = []
+            s = s + xr1[d, rows, :].astype(F32)
+        s1[j, 0:56, :] = s
+        s1[j, 56:64, :] = jnp.zeros((8, 128), F32)
+        ybuf1[j] = s1[j].astype(BF)
+    yc1 = []
+    for d in (3, 2, 4, 1, 5, 0, 6):
+        c = remote(ybuf1.at[lax.rem(y + 1 + d, 8)], yr1.at[d], yss.at[7 + d], yrs.at[7 + d], y_peers[d])
+        c.start()
+        yc1.append(c)
+    for c in yc2:
+        c.wait()
+    s = g2[y]
     for d in range(7):
-        c = remote(ybuf.at[lax.rem(y + 1 + d, 8)], yr.at[d], yss.at[d], yrs.at[d], y_peers[d])
-        c.start()
-        yc.append(c)
+        s = s + yr2[d].astype(F32)
+    for i in range(4):
+        s2[i] = s[16 * i : 16 * i + 16]
+    for i in range(4):
+        xbuf2[i] = s2[i].astype(BF)
+    xc2 = []
+    for d in (1, 0, 2):
+        c = remote(xbuf2.at[lax.rem(x + 1 + d, 4)], xr2.at[d], xss.at[3 + d], xrs.at[3 + d], x_peers[d])
+        c.start()
+        xc2.append(c)
 
     for d in range(3):
         f2[d].wait()
-    for d in range(3):
-        g2[d].wait_send()
+        g2s[d].wait_send()
 
     def back(b, _):
         at_row = 4 * b
         cells = pl.ds(pl.multiple_of(256 * b, 256), 256)
-        total = cot_sh[1, pl.ds(4 + at_row, 4)].reshape(256, 256).astype(F32)
+        total = cot24[pl.ds(4 + 8 * core + at_row, 4)].reshape(256, 256).astype(F32)
         for t in range(9):
             m, n = t // 3, t % 3
-            win = cot_sh[n, pl.ds(at_row + 8 - 4 * m, 4)].reshape(256, 256)
+            win = cot_sh[n, pl.ds(8 * core + at_row + 8 - 4 * m, 4)].reshape(256, 256)
             total = total + dot_nn(win, w2[t])
         v = pre[cells, :]
         s = 1.0 / (1.0 + jnp.exp(-v))
@@ -283,13 +330,22 @@
     lax.fori_loop(0, 2, back, 0)
     hgp = remote(gp.at[0], gp.at[8], hs.at[10], hr.at[10], up)
     hgp.start()
-
+    haedge.wait()
+    shifted(actr, aedge_r, act_sh)
+
+    for c in xc2:
+        c.wait()
+    s = s2[x]
+    for d in range(3):
+        s = s + xr2[d].astype(F32)
+    zsum[56:72, :] = s
+    for c in yc1:
+        c.wait()
+    s = s1[y, 0:56, :]
     for d in range(7):
-        yc[d].wait()
-    s = ysum[y]
-    for d in range(7):
-        s = s + yr[d].astype(F32)
-    zsum[...] = s
+        s = s + yr1[d].astype(F32)[0:56]
+    zsum[0:56, :] = s
+    zsum[72:80, :] = jnp.zeros((8, 128), F32)
     for p in range(16):
         pbuf[p] = zsum[(9 * p) // 2 : (9 * p) // 2 + 8, :]
     slot = core * 8 + rad * 4 + zlo
@@ -379,25 +435,26 @@
 
     dma = pltpu.SemaphoreType.DMA
     scratch = [
-        vm((17, 128, 256)), vm((3, 2, 9, 64, 256)), vm((32, 256), F32), vm((32, 256)), vm((32, 256)),
-        vm((9, 256, 256)), vm((9, 256, 256)), vm((16, 64, 256)), vm((3, 16, 64, 256)),
-        vm((64, 256), F32), vm((64, 256)), vm((64, 256)), vm((64, 256)), vm((64, 256)),
-        vm((16, 80, 256), F32), vm((2, 3, 16, 64, 128)), vm((16, 64, 256)), vm((2, 512, 256)),
+        vm((17, 128, 256)), vm((3, 2, 9, 64, 256)), vm((32, 256), F32), vm((16, 256)), vm((16, 256)), vm((16, 256)),
+        vm((9, 256, 256)), vm((9, 256, 256)), vm((24, 64, 256)), vm((3, 24, 64, 256)), vm((3, 24, 64, 128)),
+        vm((64, 256), F32), vm((32, 256)), vm((96, 256)), vm((64, 256)), vm((64, 256)),
+        vm((24, 80, 256), F32), vm((16, 64, 256)), vm((2, 512, 256)),
         vm((3, 16, 64, 256)), vm((512, 256), F32), vm((256, 1024)),
-        vm((4, 8, 80, 128), F32), vm((4, 8, 80, 128)), vm((3, 8, 80, 128)),
-        vm((8, 80, 128), F32), vm((8, 80, 128)), vm((7, 80, 128)),
+        vm((4, 448, 128), F32), vm((8, 64, 128), F32), vm((4, 448, 128)), vm((3, 448, 128)),
+        vm((8, 64, 128), F32), vm((8, 64, 128)), vm((7, 64, 128)), vm((8, 64, 128)), vm((7, 64, 128)),
+        vm((4, 16, 128), F32), vm((4, 16, 128)), vm((3, 16, 128)),
         vm((80, 128), F32), vm((16, 8, 128), F32), vm((16, 8, 128), F32), vm((16, 128), F32),
         vm((9, 64, 256)), vm((9, 64, 256)), vm((9, 80, 256), F32), vm((16, 256)), vm((16, 256)),
-        dma((5,)), dma((6,)), dma((6,)), dma((6,)), dma((6,)), dma((12,)), dma((12,)),
-        dma((3,)), dma((3,)), dma((7,)), dma((7,)), dma((16,)), dma((16,)),
+        dma((4,)), dma((6,)), dma((6,)), dma((6,)), dma((6,)), dma((16,)), dma((16,)),
+        dma((6,)), dma((6,)), dma((14,)), dma((14,)), dma((16,)), dma((16,)),
     ]
     enc, ing, kg = pl.pallas_call(
         kernel,
         name="section",
         out_shape=(
-            jax.ShapeDtypeStruct((8, 64, 256), BF),
-            jax.ShapeDtypeStruct((16, 128, 256), BF),
-            jax.ShapeDtypeStruct((9, 128), F32),
+            pltpu.VMEM((8, 64, 256), BF),
+            pltpu.VMEM((16, 128, 256), BF),
+            pltpu.VMEM((9, 128), F32),
         ),
         in_specs=[pl.BlockSpec(memory_space=pl.ANY)] * 4,
         out_specs=[pl.BlockSpec(memory_space=pltpu.VMEM)] * 3,

time: 64.5 us -> 56.5 us (0.88)
  Pallas kernels: 59.1 us -> 53.2 us
  local copies, waits for them, and re-layouts: 4.57 us -> 2.27 us
    pallas_call x1, Pallas kernels: 59.1 us -> 53.2 us  [body(): pl.pallas_call(kernel, name='section', out_shape=(pltpu.VMEM((8, 64, 256)...]
    unnamed x5 -> x3, local copies, waits for them, and re-layouts: 4.57 us -> 2.27 us
where the time goes in v2:
time: 56.5 us; the launch traced here: 56.1 us
  Pallas kernels  53.2 us (94%)
  local copies, waits for them, and re-layouts  2.27 us (4%)
  between operations  0.64 us (1%)
    pallas_call x1, Pallas kernels, body(): pl.pallas_call(kernel, name='section', out_shape=(pltpu.VMEM((8, 64, 256)...  53.2 us
    unnamed x3, local copies, waits for them, and re-layouts  2.27 us

profile of v2, /device:TPU:1, one launch (start us, length us, event | category | flops | bytes accessed | tf_op | source)
XLA Modules:
  0.0 56.1 jit_solution(10430092890525617762)
XLA Ops:
  0.6 53.2 %section.1 = (bf16[8,64,256]{2,1,0:T(8,128)(2,1)S(1)}, bf16[16,128,256]{2,1,0:T(8,128)(2,1)S(1)}, f32[9,128]{1,0:T(8,128)S(1)}) custom-call(bf16[16,128,256]{2,1,0:T(8,128)(2,1)} %bitcast.10, bf16[9,64,256]{2,1,0:T(8,128)(2,1)} %bitcast.11, bf16[9,64,256]{2,1,0:T(8,128)(2,1)} %bitcast.12, bf16[8,64,256]{2,1,0:T(8,128)(2,1)} %bitcast.13), custom_call_target="tpu_custom_call" | custom-call | tf_op jit(solution)/shard_map/section/pallas_call | solution.py:451
  53.8 0.7 %copy.10 = bf16[1,8,64,256]{3,2,1,0:T(8,128)(2,1)} copy(bf16[1,8,64,256]{3,2,1,0:T(8,128)(2,1)S(1)} %bitcast.8) | data formatting | bytes 524288
  54.5 1.0 %copy.11 = bf16[1,16,128,256]{3,2,1,0:T(8,128)(2,1)} copy(bf16[1,16,128,256]{3,2,1,0:T(8,128)(2,1)S(1)} %bitcast.7) | data formatting | bytes 2097152
  55.5 0.6 %copy.12 = f32[1152]{0:T(1024)} copy(f32[1152]{0:T(1024)S(1)} %bitcast.9) | data formatting | bytes 9216

commit v3 on v2

v3 whole, which is shorter than its diff:
```python
import jax
import jax.numpy as jnp
from jax import lax
from jax.experimental import pallas as pl
from jax.experimental.pallas import tpu as pltpu
from jax.sharding import PartitionSpec as P

BF = jnp.bfloat16
F32 = jnp.float32
SHIFTS = (4, 0, -4)


def dot_nt(a, b):
    return lax.dot_general(a, b, (((1,), (1,)), ((), ())), preferred_element_type=F32)


def dot_nn(a, b):
    return lax.dot_general(a, b, (((1,), (0,)), ((), ())), preferred_element_type=F32)


def kernel(
    snap_hbm, w1_hbm, w2_hbm, cot_hbm,
    enc_ref, ing_ref, kg_ref,
    snap, xs, colf, cols_s, cols_r, cols_c, w1, w2, cot24, cot_sh, edgef, cedge_s, cedge_r, aedge_s, aedge_r,
    extf, actr, act_sh, pre, at, gt, g1, g2, xbuf1, xr1, s1, ybuf1, yr1, ybuf2, yr2, s2, xbuf2, xr2,
    zcom, zsum, pbuf, prec, fin, gp, gp1, gpf, gcol_s, gcol_r, gcol_c,
    loc_sem, wsend, wrecv, wfs, wfr, wzs, wzr, hs, hr, xss, xrs, yss, yrs, zss, zrs,
):
    a = lax.axis_index("azi")
    rad = lax.axis_index("rad")
    x = lax.axis_index("batch")
    core = lax.rem(a, 2)
    zlo = lax.rem(a // 2, 4)
    y = a // 8

    def dev(azi, r, b):
        return {"azi": azi, "rad": r, "batch": b}

    def signal(target):
        pl.semaphore_signal(barrier, inc=1, device_id=target, device_id_type=pl.DeviceIdType.MESH)

    def remote(src, dst, ss, rs, target):
        return pltpu.make_async_remote_copy(
            src_ref=src, dst_ref=dst, send_sem=ss, recv_sem=rs,
            device_id=target, device_id_type=pl.DeviceIdType.MESH,
        )

    other = dev(a + 1 - 2 * core, rad, x)
    up = dev(lax.rem(a + 63, 64), rad, x)
    down = dev(lax.rem(a + 1, 64), rad, x)
    band = dev(a, 1 - rad, x)
    step = 2 * core - 1
    near = dev(lax.rem(a + 64 + step, 64), rad, x)
    far = dev(lax.rem(a + 64 + 2 * step, 64), rad, x)
    far_from = dev(lax.rem(a + 64 - 2 * step, 64), rad, x)

    zi = 4 * rad + zlo

    def along_z(by):
        z2 = lax.rem(zi + 8 + by, 8)
        return dev(y * 8 + lax.rem(z2, 4) * 2 + core, z2 // 4, x)

    z_next, z_prev = along_z(1), along_z(-1)

    def across(target):
        return dev(target["azi"], 1 - rad, x)

    x_peers = [dev(a, rad, lax.rem(x + d, 4)) for d in (1, 2, 3)]
    y_peers = [dev(lax.rem(y + d, 8) * 8 + zlo * 2 + core, rad, x) for d in range(1, 8)]
    own_home = zlo == x

    barrier = pltpu.get_barrier_semaphore()
    for target in [other, up, down, band, far_from, across(other), across(near), across(far_from), across(up), across(down), z_next, z_prev] + x_peers + y_peers:
        signal(target)
    for cs in range(2):
        for zh in range(2):
            for zl in range(4):
                is_self = own_home & (core == cs) & (rad == zh) & (zlo == zl)

                @pl.when(jnp.logical_not(is_self))
                def _():
                    signal(dev((y * 4 + zl) * 2 + cs, zh, zlo))

    def shard_rows(w):
        return w.at[:, pl.ds(pl.multiple_of(64 * x, 64), 64), :]

    def half_rows(w, xi, k):
        return w.at[:, pl.ds(pl.multiple_of(64 * xi + 32 * k, 32), 32), :]

    own_snap = pl.ds(1 + 16 * core, 16)
    lsnap = pltpu.make_async_copy(snap_hbm, snap.at[own_snap], loc_sem.at[0])
    lw1 = pltpu.make_async_copy(w1_hbm, shard_rows(w1), loc_sem.at[1])
    lw2 = pltpu.make_async_copy(w2_hbm, shard_rows(w2), loc_sem.at[2])
    own_rows = pl.ds(4 + 8 * core, 8)
    lcot = pltpu.make_async_copy(cot_hbm, cot24.at[own_rows], loc_sem.at[3])
    for c in (lcot, lsnap, lw1, lw2):
        c.start()

    def edge(tile_of, out, r):
        low = tile_of(0).astype(F32)[0:4]
        high = tile_of(48).astype(F32)[12:16]
        out[4 * r : 4 * r + 4, :] = jnp.where(rad == 0, high, low)

    lcot.wait()
    for r in range(8):
        edge(lambda c: cot24[4 + 8 * core + r, c : c + 16, :], edgef, r)
    cedge_s[...] = edgef[0:32, :].astype(BF)
    pl.semaphore_wait(barrier, jnp.where(own_home, 37, 38))

    base = pl.ds(pl.multiple_of(32 * core, 32), 32)

    def part_of(w, xi, taps, k):
        return w.at[taps, pl.ds(pl.multiple_of(64 * xi + 32 * k, 32), 32), :]

    def gather_send(w, w_hbm, taps, at_sem):
        out = {}
        for d in (0, 2, 1):
            out[d] = remote(
                w_hbm.at[taps, base, :], part_of(w, x, taps, core), wsend.at[at_sem + d], wrecv.at[at_sem + d], x_peers[d]
            )
            out[d].start()
        return out

    def hand_on(w, d, taps, at_sem):
        part = part_of(w, lax.rem(x + 3 - d, 4), taps, core)
        c = remote(part, part, wfs.at[at_sem + d], wfr.at[at_sem + d], other)
        c.start()
        return c

    every = pl.ds(0, 9)
    g1s = gather_send(w1, w1_hbm, every, 0)
    hsnap = remote(snap_hbm, snap.at[own_snap], hs.at[0], hr.at[0], other)
    hsnap.start()
    row_near = remote(snap_hbm.at[15], snap.at[0], hs.at[6], hr.at[6], near)
    row_far = remote(snap_hbm.at[15], snap.at[0], hs.at[7], hr.at[6], far)

    @pl.when(core == 1)
    def _():
        row_near.start()
        row_far.start()

    edge_rows = pl.ds(4 * core, 4)
    far_rows = pl.ds(20 * (1 - core), 4)
    cot_halo = [
        remote(cot_hbm.at[edge_rows], cot24.at[far_rows], hs.at[1], hr.at[1], near),
        remote(cot_hbm.at[edge_rows], cot24.at[far_rows], hs.at[2], hr.at[2], far),
        remote(cot_hbm, cot24.at[own_rows], hs.at[4], hr.at[4], other),
    ]
    mid = pl.ds(pl.multiple_of(16 + 32 * core, 16), 32)
    tip = pl.ds(pl.multiple_of(80 * (1 - core), 16), 16)
    tip_s = pl.ds(pl.multiple_of(16 * core, 16), 16)
    for i, target in ((12, band), (13, across(other))):
        cot_halo.append(remote(cedge_s, cedge_r.at[mid], hs.at[i], hr.at[i], target))
    for i, target in ((14, across(near)), (15, across(far))):
        cot_halo.append(remote(cedge_s.at[tip_s], cedge_r.at[tip], hs.at[i], hr.at[i], target))
    for c in cot_halo:
        c.start()

    row_i = lax.broadcasted_iota(jnp.int32, (192, 128), 0)
    col_i = lax.broadcasted_iota(jnp.int32, (192, 128), 1)
    pick = jnp.where(col_i == 2 * lax.rem(row_i, 64) + row_i // 64 - 1, 1.0, 0.0).astype(BF)

    lsnap.wait()
    for r in range(16):
        e = 16 * core + 1 + r
        got = dot_nn(pick, snap[e])
        for n in range(3):
            xs[n, (1 + r) % 2, 8 * core + (1 + r) // 2] = got[64 * n : 64 * n + 64].astype(BF)
        colf[r : r + 1, :] = got[191:192]
    cols_s[...] = colf[0:16, :].astype(BF)
    col_rows = pl.ds(pl.multiple_of(16 * core, 16), 16)
    hcols = [
        remote(cols_s, cols_r.at[col_rows], hs.at[3], hr.at[3], band),
        remote(cols_s, cols_r.at[col_rows], hs.at[5], hr.at[5], across(other)),
    ]
    for c in hcols:
        c.start()
    tip_near = remote(cols_s, cols_c, hs.at[8], hr.at[8], across(near))
    tip_far = remote(cols_s, cols_c, hs.at[18], hr.at[8], across(far))

    @pl.when(core == 1)
    def _():
        tip_near.start()
        tip_far.start()

    for c in cot_halo:
        c.wait()
    got = cedge_r[...].astype(F32)
    for r in range(24):
        extf[r, 8:72, :] = cot24[r].astype(F32)
        part = got[4 * r : 4 * r + 4]
        extf[r, 4:8, :] = jnp.where(rad == 1, part, 0.0)
        extf[r, 72:76, :] = jnp.where(rad == 0, part, 0.0)
        for n, start in ((0, 12), (1, 8), (2, 4)):
            cot_sh[n, r] = extf[r, start : start + 64, :].astype(BF)

    hsnap.wait()
    for r in range(16):
        e = 16 * (1 - core) + 1 + r
        got = dot_nn(pick, snap[e])
        for n in range(3):
            xs[n, (1 + r) % 2, 8 * (1 - core) + (1 + r) // 2] = got[64 * n : 64 * n + 64].astype(BF)
    row_near.wait_recv()
    got = dot_nn(pick, snap[0])
    for n in range(3):
        xs[n, 0, 0] = got[64 * n : 64 * n + 64].astype(BF)
    for c in hcols:
        c.wait()
    tip_near.wait_recv()
    in_row = lax.broadcasted_iota(jnp.int32, (16, 256), 0)
    colv = jnp.where(rad == 1, cols_r[...].astype(F32), 0.0)
    corner = jnp.where(rad == 1, cols_c[...].astype(F32), 0.0)
    for e in range(33):
        tile = xs[0, e % 2, e // 2, 0:16, :].astype(F32)
        side = colv[e - 1 : e] if e else corner[15:16]
        xs[0, e % 2, e // 2, 0:16, :] = jnp.where(in_row == 0, side, tile).astype(BF)
    lw1.wait()
    f1 = []
    for d in (0, 2, 1):
        g1s[d].wait_recv()
    for d in (0, 2, 1):
        f1.append(hand_on(w1, d, every, 0))
    even = lax.rem(zlo, 2)

    def quarter(w, xi, taps):
        return w.at[taps, pl.ds(pl.multiple_of(64 * xi + 32 * core + 16 * even, 16), 16), :]

    g2s = {}
    for d in (0, 2, 1):
        g2s[d] = remote(
            w2_hbm.at[every, pl.ds(pl.multiple_of(32 * core + 16 * even, 16), 16), :],
            quarter(w2, x, every), wsend.at[3 + d], wrecv.at[3 + d], x_peers[d],
        )
        g2s[d].start()

    def edges(field, out):
        for r in range(16):
            edge(lambda c: field[r, c : c + 16, :], edgef, r)
        out[...] = edgef[...].astype(BF)

    def shifted(field, edge_got, sh):
        got = edge_got[...].astype(F32)
        for r in range(16):
            extf[r, 8:72, :] = field[r].astype(F32)
            part = got[4 * r : 4 * r + 4]
            extf[r, 4:8, :] = jnp.where(rad == 1, part, 0.0)
            extf[r, 72:76, :] = jnp.where(rad == 0, part, 0.0)
            sh[1, r] = field[r]
            sh[2, r] = extf[r, 4:68, :].astype(BF)
            sh[0, r] = extf[r, 12:76, :].astype(BF)

    def conv1(b, _):
        total = jnp.zeros((256, 128), F32)
        for t in range(9):
            m, n = t // 3, t % 3
            win = xs[n, m % 2, pl.ds(4 * b + m // 2, 4)].reshape(256, 256)
            w = jnp.concatenate(
                [w1[t, pl.ds(pl.multiple_of(64 * i + 32 * core, 32), 32), :] for i in range(4)], axis=0
            )
            total = total + dot_nt(win, w)
        sig = 1.0 / (1.0 + jnp.exp(-total))
        at[:, pl.ds(pl.multiple_of(256 * b, 256), 256)] = (total * sig).astype(BF).T
        return 0

    lax.fori_loop(0, 4, conv1, 0, unroll=True)
    def tiles_before(tile, k):
        q = tile // 9
        return sum((u // 4) % 2 == k for u in range(9 * q, tile))

    xc1 = []
    for chunk, taps in enumerate(((0, 1, 2), (3, 4), (5, 6), (7, 8))):
        for t in taps:
            m, n = t // 3, t % 3
            win = cot_sh[n, 8 - 4 * m : 24 - 4 * m].reshape(1024, 256)
            gt[t] = dot_nn(at[...], win) * (1.0 / 512.0)
        for k in range(2):
            @pl.when(core == k)
            def _():
                for tile in range(72 * chunk, 72 * chunk + 72):
                    if (tile // 4) % 2 != k:
                        continue
                    q, c = tile // 9, tiles_before(tile, k)
                    t, within = tile // 32, tile % 32
                    i = 4 * (within // 8) + within % 4
                    rows = gt[t, 8 * i : 8 * i + 8, :]
                    if c < 4:
                        g1[q % 4, 32 * (q // 4) + 8 * c : 32 * (q // 4) + 8 * c + 8, :] = rows
                    else:
                        g2[q // 4, 8 * (q % 4) : 8 * (q % 4) + 8, :] = rows
                for q in range(8 * chunk, 8 * chunk + 8):
                    if sum((u // 4) % 2 == k for u in range(9 * q, 9 * q + 9)) < 5:
                        g2[q // 4, 8 * (q % 4) : 8 * (q % 4) + 8, :] = jnp.zeros((8, 256), F32)

        some = slice(64 * chunk, 64 * chunk + 64)
        for i in range(4):
            xbuf1[i, some, :] = g1[i, some, :].astype(BF)
        for d in (1, 0, 2):
            c = remote(
                xbuf1.at[lax.rem(x + 1 + d, 4), pl.ds(64 * chunk, 64)], xr1.at[d, pl.ds(64 * chunk, 64)],
                xss.at[3 * chunk + d], xrs.at[3 * chunk + d], x_peers[d],
            )
            c.start()
            xc1.append(c)
    for i in range(8):
        ybuf2[i] = g2[i].astype(BF)
    yc2 = []
    for d in (3, 2, 4, 1, 5, 0, 6):
        c = remote(ybuf2.at[lax.rem(y + 1 + d, 8)], yr2.at[d], yss.at[d], yrs.at[d], y_peers[d])
        c.start()
        yc2.append(c)

    for c in f1:
        c.wait()
    for d in range(3):
        g1s[d].wait_send()

    def own(b, _):
        at_row = 4 * b
        total = jnp.zeros((256, 256), F32)
        for t in range(9):
            m, n = t // 3, t % 3
            win = xs[n, m % 2, pl.ds(8 * core + at_row + m // 2, 4)].reshape(256, 256)
            total = total + dot_nt(win, w1[t])
        pre[pl.ds(pl.multiple_of(256 * b, 256), 256), :] = total
        sig = 1.0 / (1.0 + jnp.exp(-total))
        actr[pl.ds(4 + at_row, 4)] = (total * sig).astype(BF).reshape(4, 64, 256)
        return 0

    lax.fori_loop(0, 2, own, 0)
    hact_u = remote(actr.at[4:8], actr.at[12:16], hs.at[16], hr.at[16], up)
    hact_u.start()
    hact_d = remote(actr.at[8:12], actr.at[0:4], hs.at[19], hr.at[19], down)
    hact_d.start()
    by_z = []
    for d in (0, 2, 1):
        g2s[d].wait_recv()
        for i, (taps, target) in enumerate(((pl.ds(0, 5), z_next), (pl.ds(5, 4), z_prev))):
            part = quarter(w2, lax.rem(x + 3 - d, 4), taps)
            c = remote(part, part, wzs.at[2 * d + i], wzr.at[2 * d + i], target)
            c.start()
            by_z.append(c)
    f2 = []
    for i, d in enumerate((0, 2, 1)):
        by_z[2 * i].wait_recv()
        by_z[2 * i + 1].wait_recv()
        f2.append(hand_on(w2, d, every, 3))
    lw2.wait()

    yc1 = []
    for chunk in range(4):
        for c in xc1[3 * chunk : 3 * chunk + 3]:
            c.wait()
        for j in (2 * chunk, 2 * chunk + 1):
            rows = slice(32 * j, 32 * j + 32)
            s = g1[x, rows, :]
            for d in range(3):
                s = s + xr1[d, rows, :].astype(F32)
            s1[j] = s
            ybuf1[j] = s.astype(BF)
            d = lax.rem(j + 7 - y + 8, 8)

            @pl.when(y != j)
            def _():
                remote(
                    ybuf1.at[j], yr1.at[d], yss.at[7 + d], yrs.at[7 + d], dev(j * 8 + zlo * 2 + core, rad, x)
                ).start()
    for d in range(7):
        yc1.append(remote(ybuf1.at[0], yr1.at[d], yss.at[7 + d], yrs.at[7 + d], y_peers[d]))
    for c in yc2:
        c.wait()
    s = g2[y]
    for d in range(7):
        s = s + yr2[d].astype(F32)
    for i in range(4):
        s2[i, 0:8, :] = s[8 * i : 8 * i + 8]
        s2[i, 8:16, :] = jnp.zeros((8, 256), F32)
    for i in range(4):
        xbuf2[i] = s2[i].astype(BF)
    xc2 = []
    for d in (1, 0, 2):
        c = remote(xbuf2.at[lax.rem(x + 1 + d, 4)], xr2.at[d], xss.at[12 + d], xrs.at[12 + d], x_peers[d])
        c.start()
        xc2.append(c)

    hact_d.wait()
    hact_u.wait()
    edges(actr, aedge_s)
    haedge = remote(aedge_s, aedge_r, hs.at[9], hr.at[9], band)
    haedge.start()
    for d in range(3):
        f2[d].wait()
        g2s[d].wait_send()
        by_z[2 * d].wait_send()
        by_z[2 * d + 1].wait_send()

    def back(b, _):
        at_row = 4 * b
        cells = pl.ds(pl.multiple_of(256 * b, 256), 256)
        total = cot24[pl.ds(4 + 8 * core + at_row, 4)].reshape(256, 256).astype(F32)
        for t in range(9):
            m, n = t // 3, t % 3
            win = cot_sh[n, pl.ds(8 * core + at_row + 8 - 4 * m, 4)].reshape(256, 256)
            total = total + dot_nn(win, w2[t])
        v = pre[cells, :]
        s = 1.0 / (1.0 + jnp.exp(-v))
        g = (total * (s * (1.0 + v * (1.0 - s)))).astype(BF)
        gp[pl.ds(at_row, 4)] = g.reshape(4, 64, 256)
        for i in range(4):
            colf[pl.ds(at_row + i, 1), :] = g[64 * i : 64 * i + 16].astype(F32)[0:1]
        return 0

    lax.fori_loop(0, 2, back, 0)
    gcol_s[...] = colf[0:16, :].astype(BF)
    hgp = [
        remote(gp.at[0], gp.at[8], hs.at[10], hr.at[10], up),
        remote(gcol_s, gcol_r, hs.at[11], hr.at[11], band),
        remote(gcol_s, gcol_c, hs.at[17], hr.at[17], across(up)),
    ]
    for c in hgp:
        c.start()

    for c in xc2:
        c.wait()
    s = s2[x]
    for d in range(3):
        s = s + xr2[d].astype(F32)
    zcom[4] = s[0:8]
    for c in yc1:
        c.wait()
    s = s1[y]
    for d in range(7):
        s = s + yr1[d].astype(F32)
    for i in range(4):
        zcom[i] = s[8 * i : 8 * i + 8]
    phase = lax.rem(4 * y + x, 8)
    before = 0
    for u in range(9):
        held = lax.rem((phase + u) // 4, 2) == core
        tile = zcom[before if u == 0 else jnp.minimum(before, 4)]
        zsum[8 * u : 8 * u + 8, :] = jnp.where(held, tile, 0.0)
        before = before + jnp.where(held, 1, 0)
    zsum[72:80, :] = jnp.zeros((8, 256), F32)
    for p in range(16):
        rows = zsum[(9 * p) // 2 : (9 * p) // 2 + 8, :]
        pbuf[p] = jnp.concatenate([rows[:, 0:128], rows[:, 128:256]], axis=0).astype(BF)
    slot = core * 8 + rad * 4 + zlo
    zc = []
    for p in range(16):
        c1, zh, xp = p // 8, (p // 4) % 2, p % 4
        is_self = own_home & (core == c1) & (rad == zh) & (x == xp)
        rc = remote(pbuf.at[p], prec.at[slot], zss.at[p], zrs.at[slot], dev((y * 4 + x) * 2 + c1, zh, xp))
        lc = pltpu.make_async_copy(pbuf.at[p], prec.at[slot], zrs.at[slot])

        @pl.when(is_self)
        def _():
            lc.start()

        @pl.when(jnp.logical_not(is_self))
        def _():
            rc.start()

        zc.append((is_self, rc))

    haedge.wait()
    shifted(actr, aedge_r, act_sh)

    def ahead(b, _):
        at_row = 4 * b
        total = act_sh[1, pl.ds(4 + at_row, 4)].reshape(256, 256).astype(F32)
        for t in range(9):
            m, n = t // 3, t % 3
            win = act_sh[2 - n, pl.ds(at_row + 4 * m, 4)].reshape(256, 256)
            total = total + dot_nt(win, w2[t])
        enc_ref[pl.ds(at_row, 4)] = total.astype(BF).reshape(4, 64, 256)
        return 0

    lax.fori_loop(0, 2, ahead, 0)
    for c in hgp:
        c.wait()
    colv = jnp.where(rad == 0, gcol_r[...].astype(F32), 0.0)
    corner = jnp.where(rad == 0, gcol_c[...].astype(F32), 0.0)
    for r in range(9):
        gpf[r, 0:64, :] = gp[r].astype(F32)
        gpf[r, 64:65, :] = colv[r : r + 1] if r < 8 else corner[0:1]
        gp1[r] = gpf[r, 1:65, :].astype(BF)

    row_q = lax.broadcasted_iota(jnp.int32, (128, 128), 0)
    col_q = lax.broadcasted_iota(jnp.int32, (128, 128), 1)
    weave = jnp.where(col_q == lax.rem(row_q, 2) * 64 + row_q // 2, 1.0, 0.0).astype(BF)
    ptaps = (((1, 0),), ((2, 0), (0, 1)))

    def inward(b, _):
        at_row = 4 * b
        for rp in range(2):
            halves = []
            for cp in range(2):
                total = jnp.zeros((256, 256), F32)
                for m, rs in ptaps[rp]:
                    for n, cs in ptaps[cp]:
                        field = gp1 if cs else gp
                        win = field[pl.ds(at_row + rs, 4)].reshape(256, 256)
                        total = total + dot_nn(win, w1[3 * m + n])
                halves.append(total.astype(BF).reshape(4, 64, 256))
            for i in range(4):
                pair = jnp.concatenate([halves[0][i], halves[1][i]], axis=0)
                ing_ref[2 * (at_row + i) + rp] = dot_nn(weave, pair).astype(BF)
        return 0

    lax.fori_loop(0, 2, inward, 0)
    @pl.when(core == 1)
    def _():
        for c in (row_near, row_far, tip_near, tip_far):
            c.wait_send()


    for s in range(16):
        pltpu.make_async_copy(pbuf.at[0], prec.at[s], zrs.at[s]).wait()
    s = prec[0].astype(F32)
    for i in range(1, 16):
        s = s + prec[i].astype(F32)
    for i in range(5):
        fin[2 * i : 2 * i + 1, :] = s[i : i + 1]
        fin[2 * i + 1 : 2 * i + 2, :] = s[8 + i : 9 + i]
    result = jnp.where(lax.rem(x, 2) == 0, fin[0:9, :], fin[1:10, :])
    for i in range(9):
        kg_ref[128 * i : 128 * i + 128] = result[i]
    for is_self, rc in zc:
        @pl.when(jnp.logical_not(is_self))
        def _():
            rc.wait_send()


def closing(enc_in, ing_in, kg_in, enc_out, ing_out, kg_out, sem):
    copies = [
        pltpu.make_async_copy(src, dst, sem.at[i])
        for i, (src, dst) in enumerate(((ing_in, ing_out), (enc_in, enc_out), (kg_in, kg_out)))
    ]
    for c in copies:
        c.start()
    for c in copies:
        c.wait()


def body(snapshots, first_kernel, second_kernel, cotangent):
    def vm(shape, kind=BF):
        return pltpu.VMEM(shape, kind)

    dma = pltpu.SemaphoreType.DMA
    scratch = [
        vm((33, 128, 256)), vm((3, 2, 17, 64, 256)), vm((40, 256), F32), vm((16, 256)), vm((32, 256)), vm((16, 256)),
        vm((9, 256, 256)), vm((9, 256, 256)), vm((24, 64, 256)), vm((3, 24, 64, 256)),
        vm((64, 256), F32), vm((32, 256)), vm((96, 256)), vm((64, 256)), vm((64, 256)),
        vm((24, 80, 256), F32), vm((16, 64, 256)),
        vm((3, 16, 64, 256)), vm((512, 256), F32), vm((128, 1024)), vm((9, 128, 256), F32),
        vm((4, 256, 256), F32), vm((8, 32, 256), F32), vm((4, 256, 256)), vm((3, 256, 256)),
        vm((8, 32, 256), F32), vm((8, 32, 256)), vm((7, 32, 256)), vm((8, 32, 256)), vm((7, 32, 256)),
        vm((4, 16, 256), F32), vm((4, 16, 256)), vm((3, 16, 256)),
        vm((5, 8, 256), F32), vm((80, 256), F32), vm((16, 16, 128)), vm((16, 16, 128)), vm((16, 128), F32),
        vm((9, 64, 256)), vm((9, 64, 256)), vm((9, 80, 256), F32), vm((16, 256)), vm((16, 256)), vm((16, 256)),
        dma((4,)), dma((6,)), dma((6,)), dma((6,)), dma((6,)), dma((6,)), dma((6,)), dma((20,)), dma((20,)),
        dma((15,)), dma((15,)), dma((14,)), dma((14,)), dma((16,)), dma((16,)),
    ]
    enc, ing, kg = pl.pallas_call(
        kernel,
        name="section",
        out_shape=(
            pltpu.VMEM((8, 64, 256), BF),
            pltpu.VMEM((16, 128, 256), BF),
            pltpu.VMEM((1152,), F32),
        ),
        in_specs=[pl.BlockSpec(memory_space=pl.ANY)] * 4,
        out_specs=[pl.BlockSpec(memory_space=pltpu.VMEM)] * 3,
        scratch_shapes=scratch,
        compiler_params=pltpu.CompilerParams(
            collective_id=0, has_side_effects=True, vmem_limit_bytes=56 << 20
        ),
    )(
        snapshots[0],
        jnp.swapaxes(first_kernel, 1, 2),
        jnp.swapaxes(second_kernel, 1, 2),
        cotangent[0],
    )
    enc, ing, kg = pl.pallas_call(
        closing,
        name="closing",
        out_shape=(
            jax.ShapeDtypeStruct((8, 64, 256), BF),
            jax.ShapeDtypeStruct((16, 128, 256), BF),
            jax.ShapeDtypeStruct((1152,), F32),
        ),
        in_specs=[pl.BlockSpec(memory_space=pl.ANY)] * 3,
        out_specs=[pl.BlockSpec(memory_space=pl.ANY)] * 3,
        scratch_shapes=[dma((3,))],
        compiler_params=pltpu.CompilerParams(vmem_limit_bytes=1 << 20),
    )(enc, ing, kg)
    return enc[None], ing[None], kg


def solution(mesh):
    return jax.shard_map(
        body,
        mesh=mesh,
        in_specs=(
            P("batch", "azi", "rad", None),
            P(None, None, "batch"),
            P(None, None, "batch"),
            P("batch", "azi", "rad", None),
        ),
        out_specs=(
            P("batch", "azi", "rad", None),
            P("batch", "azi", "rad", None),
            P(("azi", "rad", "batch")),
        ),
        check_vma=False,
    )
```

time: 56.5 us -> 55.5 us (0.982)
  local copies, waits for them, and re-layouts: 2.27 us -> 0 us
  Pallas kernels: 53.2 us -> 54.7 us
    unnamed x3 -> x0, local copies, waits for them, and re-layouts: 2.27 us -> none
    pallas_call x0 -> x1, Pallas kernels: none -> 1.08 us  [body(): pl.pallas_call(closing, name='closing', out_shape=(jax.ShapeDtypeStruct((...]
where the time goes in v3:
time: 55.5 us; the launch traced here: 55.4 us
  Pallas kernels  54.7 us (99%)
  between operations  0.64 us (1%)
    pallas_call x1, Pallas kernels, body(): pl.pallas_call(kernel, name='section', out_shape=(pltpu.VMEM((8, 64, 256)...  53.7 us

profile of v3, /device:TPU:1, one launch (start us, length us, event | category | flops | bytes accessed | tf_op | source)
XLA Modules:
  0.0 55.4 jit_solution(6489688581594012867)
XLA Ops:
  0.6 53.7 %section.1 = (bf16[8,64,256]{2,1,0:T(8,128)(2,1)S(1)}, bf16[16,128,256]{2,1,0:T(8,128)(2,1)S(1)}, f32[1152]{0:T(1024)S(1)}) custom-call(bf16[16,128,256]{2,1,0:T(8,128)(2,1)} %bitcast.6, bf16[9,64,256]{2,1,0:T(8,128)(2,1)} %bitcast.7, bf16[9,64,256]{2,1,0:T(8,128)(2,1)} %bitcast.8, bf16[8,64,256]{2,1,0:T(8,128)(2,1)} %bitcast.9), custom_call_target="tpu_custom_call" | custom-call | tf_op jit(solution)/shard_map/section/pallas_call | solution.py:563
  54.3 1.1 %closing.1 = (bf16[8,64,256]{2,1,0:T(8,128)(2,1)}, bf16[16,128,256]{2,1,0:T(8,128)(2,1)}, f32[1152]{0:T(1024)}) custom-call(bf16[8,64,256]{2,1,0:T(8,128)(2,1)S(1)} %get-tuple-element.9.enc_in, bf16[16,128,256]{2,1,0:T(8,128)(2,1)S(1)} %get-tuple-element.10.ing_in, f32[1152]{0:T(1024)S(1)} %get-tuple-element.11.kg_in), custom_call_target="tpu_custom_call" | custom-call | tf_op jit(solution)/shard_map/closing/pallas_call | solution.py:583

commit v4 on v3

--- a/solution.py
+++ b/solution.py
@@ -51,8 +51,6 @@
     band = dev(a, 1 - rad, x)
     step = 2 * core - 1
     near = dev(lax.rem(a + 64 + step, 64), rad, x)
-    far = dev(lax.rem(a + 64 + 2 * step, 64), rad, x)
-    far_from = dev(lax.rem(a + 64 - 2 * step, 64), rad, x)
 
     zi = 4 * rad + zlo
 
@@ -70,7 +68,7 @@
     own_home = zlo == x
 
     barrier = pltpu.get_barrier_semaphore()
-    for target in [other, up, down, band, far_from, across(other), across(near), across(far_from), across(up), across(down), z_next, z_prev] + x_peers + y_peers:
+    for target in [other, up, down, band, across(near), across(up), across(down), z_next, z_prev] + x_peers + y_peers:
         signal(target)
     for cs in range(2):
         for zh in range(2):
@@ -105,7 +103,7 @@
     for r in range(8):
         edge(lambda c: cot24[4 + 8 * core + r, c : c + 16, :], edgef, r)
     cedge_s[...] = edgef[0:32, :].astype(BF)
-    pl.semaphore_wait(barrier, jnp.where(own_home, 37, 38))
+    pl.semaphore_wait(barrier, jnp.where(own_home, 34, 35))
 
     base = pl.ds(pl.multiple_of(32 * core, 32), 32)
 
@@ -132,29 +130,32 @@
     hsnap = remote(snap_hbm, snap.at[own_snap], hs.at[0], hr.at[0], other)
     hsnap.start()
     row_near = remote(snap_hbm.at[15], snap.at[0], hs.at[6], hr.at[6], near)
-    row_far = remote(snap_hbm.at[15], snap.at[0], hs.at[7], hr.at[6], far)
+    row_pass = remote(snap.at[0], snap.at[0], hs.at[7], hr.at[7], other)
 
     @pl.when(core == 1)
     def _():
         row_near.start()
-        row_far.start()
 
     edge_rows = pl.ds(4 * core, 4)
     far_rows = pl.ds(20 * (1 - core), 4)
-    cot_halo = [
-        remote(cot_hbm.at[edge_rows], cot24.at[far_rows], hs.at[1], hr.at[1], near),
-        remote(cot_hbm.at[edge_rows], cot24.at[far_rows], hs.at[2], hr.at[2], far),
-        remote(cot_hbm, cot24.at[own_rows], hs.at[4], hr.at[4], other),
-    ]
     mid = pl.ds(pl.multiple_of(16 + 32 * core, 16), 32)
     tip = pl.ds(pl.multiple_of(80 * (1 - core), 16), 16)
     tip_s = pl.ds(pl.multiple_of(16 * core, 16), 16)
-    for i, target in ((12, band), (13, across(other))):
-        cot_halo.append(remote(cedge_s, cedge_r.at[mid], hs.at[i], hr.at[i], target))
-    for i, target in ((14, across(near)), (15, across(far))):
-        cot_halo.append(remote(cedge_s.at[tip_s], cedge_r.at[tip], hs.at[i], hr.at[i], target))
+    cot_halo = [
+        remote(cot_hbm.at[edge_rows], cot24.at[far_rows], hs.at[1], hr.at[1], near),
+        remote(cedge_s, cedge_r.at[mid], hs.at[12], hr.at[12], band),
+        remote(cedge_s.at[tip_s], cedge_r.at[tip], hs.at[14], hr.at[14], across(near)),
+        remote(cot_hbm, cot24.at[own_rows], hs.at[4], hr.at[4], other),
+    ]
     for c in cot_halo:
         c.start()
+    got_rows = cot24.at[pl.ds(20 * core, 4)]
+    got_tip = cedge_r.at[pl.ds(pl.multiple_of(80 * core, 16), 16)]
+    cot_pass = [
+        remote(got_rows, got_rows, hs.at[2], hr.at[2], other),
+        remote(cedge_r.at[mid], cedge_r.at[mid], hs.at[13], hr.at[13], other),
+        remote(got_tip, got_tip, hs.at[15], hr.at[15], other),
+    ]
 
     row_i = lax.broadcasted_iota(jnp.int32, (192, 128), 0)
     col_i = lax.broadcasted_iota(jnp.int32, (192, 128), 1)
@@ -169,30 +170,15 @@
         colf[r : r + 1, :] = got[191:192]
     cols_s[...] = colf[0:16, :].astype(BF)
     col_rows = pl.ds(pl.multiple_of(16 * core, 16), 16)
-    hcols = [
-        remote(cols_s, cols_r.at[col_rows], hs.at[3], hr.at[3], band),
-        remote(cols_s, cols_r.at[col_rows], hs.at[5], hr.at[5], across(other)),
-    ]
-    for c in hcols:
-        c.start()
+    hcols = remote(cols_s, cols_r.at[col_rows], hs.at[3], hr.at[3], band)
+    hcols.start()
+    cols_pass = remote(cols_r.at[col_rows], cols_r.at[col_rows], hs.at[5], hr.at[5], other)
     tip_near = remote(cols_s, cols_c, hs.at[8], hr.at[8], across(near))
-    tip_far = remote(cols_s, cols_c, hs.at[18], hr.at[8], across(far))
+    tip_pass = remote(cols_c, cols_c, hs.at[18], hr.at[18], other)
 
     @pl.when(core == 1)
     def _():
         tip_near.start()
-        tip_far.start()
-
-    for c in cot_halo:
-        c.wait()
-    got = cedge_r[...].astype(F32)
-    for r in range(24):
-        extf[r, 8:72, :] = cot24[r].astype(F32)
-        part = got[4 * r : 4 * r + 4]
-        extf[r, 4:8, :] = jnp.where(rad == 1, part, 0.0)
-        extf[r, 72:76, :] = jnp.where(rad == 0, part, 0.0)
-        for n, start in ((0, 12), (1, 8), (2, 4)):
-            cot_sh[n, r] = extf[r, start : start + 64, :].astype(BF)
 
     hsnap.wait()
     for r in range(16):
@@ -200,13 +186,48 @@
         got = dot_nn(pick, snap[e])
         for n in range(3):
             xs[n, (1 + r) % 2, 8 * (1 - core) + (1 + r) // 2] = got[64 * n : 64 * n + 64].astype(BF)
-    row_near.wait_recv()
+    for d in (0, 2, 1):
+        g1s[d].wait_recv()
+    even = lax.rem(zlo, 2)
+
+    def quarter(w, xi, taps):
+        return w.at[taps, pl.ds(pl.multiple_of(64 * xi + 32 * core + 16 * even, 16), 16), :]
+
+    g2s = {}
+    for d in (0, 2, 1):
+        g2s[d] = remote(
+            w2_hbm.at[every, pl.ds(pl.multiple_of(32 * core + 16 * even, 16), 16), :],
+            quarter(w2, x, every), wsend.at[3 + d], wrecv.at[3 + d], x_peers[d],
+        )
+        g2s[d].start()
+
+    @pl.when(core == 0)
+    def _():
+        row_near.wait_recv()
+        row_pass.start()
+        tip_near.wait_recv()
+        tip_pass.start()
+
+    hcols.wait()
+    cols_pass.start()
+    for i in range(3):
+        cot_halo[i].wait_recv()
+        cot_pass[i].start()
+    f1 = []
+    for d in (0, 2, 1):
+        f1.append(hand_on(w1, d, every, 0))
+
+    @pl.when(core == 1)
+    def _():
+        row_pass.wait_recv()
+        tip_pass.wait_recv()
+        row_near.wait_send()
+        tip_near.wait_send()
+
     got = dot_nn(pick, snap[0])
     for n in range(3):
         xs[n, 0, 0] = got[64 * n : 64 * n + 64].astype(BF)
-    for c in hcols:
-        c.wait()
-    tip_near.wait_recv()
+    cols_pass.wait()
     in_row = lax.broadcasted_iota(jnp.int32, (16, 256), 0)
     colv = jnp.where(rad == 1, cols_r[...].astype(F32), 0.0)
     corner = jnp.where(rad == 1, cols_c[...].astype(F32), 0.0)
@@ -215,23 +236,6 @@
         side = colv[e - 1 : e] if e else corner[15:16]
         xs[0, e % 2, e // 2, 0:16, :] = jnp.where(in_row == 0, side, tile).astype(BF)
     lw1.wait()
-    f1 = []
-    for d in (0, 2, 1):
-        g1s[d].wait_recv()
-    for d in (0, 2, 1):
-        f1.append(hand_on(w1, d, every, 0))
-    even = lax.rem(zlo, 2)
-
-    def quarter(w, xi, taps):
-        return w.at[taps, pl.ds(pl.multiple_of(64 * xi + 32 * core + 16 * even, 16), 16), :]
-
-    g2s = {}
-    for d in (0, 2, 1):
-        g2s[d] = remote(
-            w2_hbm.at[every, pl.ds(pl.multiple_of(32 * core + 16 * even, 16), 16), :],
-            quarter(w2, x, every), wsend.at[3 + d], wrecv.at[3 + d], x_peers[d],
-        )
-        g2s[d].start()
 
     def edges(field, out):
         for r in range(16):
@@ -263,6 +267,21 @@
         return 0
 
     lax.fori_loop(0, 4, conv1, 0, unroll=True)
+
+    for c in cot_pass:
+        c.wait()
+    cot_halo[3].wait()
+    for c in cot_halo[0:3]:
+        c.wait_send()
+    got = cedge_r[...].astype(F32)
+    for r in range(24):
+        extf[r, 8:72, :] = cot24[r].astype(F32)
+        part = got[4 * r : 4 * r + 4]
+        extf[r, 4:8, :] = jnp.where(rad == 1, part, 0.0)
+        extf[r, 72:76, :] = jnp.where(rad == 0, part, 0.0)
+        for n, start in ((0, 12), (1, 8), (2, 4)):
+            cot_sh[n, r] = extf[r, start : start + 64, :].astype(BF)
+
     def tiles_before(tile, k):
         q = tile // 9
         return sum((u // 4) % 2 == k for u in range(9 * q, tile))
@@ -507,10 +526,11 @@
         return 0
 
     lax.fori_loop(0, 2, inward, 0)
-    @pl.when(core == 1)
+
+    @pl.when(core == 0)
     def _():
-        for c in (row_near, row_far, tip_near, tip_far):
-            c.wait_send()
+        row_pass.wait_send()
+        tip_pass.wait_send()
 
 
     for s in range(16):

time: 55.5 us -> 50.7 us (0.914)
  Pallas kernels: 54.7 us -> 50 us
    pallas_call x1, Pallas kernels: 53.7 us -> 48.9 us  [body(): pl.pallas_call(kernel, name='section', out_shape=(pltpu.VMEM((8, 64, 256)...]
where the time goes in v4:
time: 50.7 us; the launch traced here: 50.6 us
  Pallas kernels  50 us (99%)
  between operations  0.64 us (1%)
    pallas_call x1, Pallas kernels, body(): pl.pallas_call(kernel, name='section', out_shape=(pltpu.VMEM((8, 64, 256)...  48.9 us
    pallas_call x1, Pallas kernels, body(): pl.pallas_call(closing, name='closing', out_shape=(jax.ShapeDtypeStruct((...  1.08 us

profile of v4, /device:TPU:1, one launch (start us, length us, event | category | flops | bytes accessed | tf_op | source)
XLA Modules:
  0.0 50.6 jit_solution(16963490696087531122)
XLA Ops:
  0.6 48.9 %section.1 = (bf16[8,64,256]{2,1,0:T(8,128)(2,1)S(1)}, bf16[16,128,256]{2,1,0:T(8,128)(2,1)S(1)}, f32[1152]{0:T(1024)S(1)}) custom-call(bf16[16,128,256]{2,1,0:T(8,128)(2,1)} %bitcast.6, bf16[9,64,256]{2,1,0:T(8,128)(2,1)} %bitcast.7, bf16[9,64,256]{2,1,0:T(8,128)(2,1)} %bitcast.8, bf16[8,64,256]{2,1,0:T(8,128)(2,1)} %bitcast.9), custom_call_target="tpu_custom_call" | custom-call | tf_op jit(solution)/shard_map/section/pallas_call | solution.py:583
  49.5 1.1 %closing.1 = (bf16[8,64,256]{2,1,0:T(8,128)(2,1)}, bf16[16,128,256]{2,1,0:T(8,128)(2,1)}, f32[1152]{0:T(1024)}) custom-call(bf16[8,64,256]{2,1,0:T(8,128)(2,1)S(1)} %get-tuple-element.9.enc_in, bf16[16,128,256]{2,1,0:T(8,128)(2,1)S(1)} %get-tuple-element.10.ing_in, f32[1152]{0:T(1024)S(1)} %get-tuple-element.11.kg_in), custom_call_target="tpu_custom_call" | custom-call | tf_op jit(solution)/shard_map/closing/pallas_call | solution.py:603

commit v5 on v4

--- a/solution.py
+++ b/solution.py
@@ -328,6 +328,15 @@
         c.start()
         yc2.append(c)
 
+    by_z = []
+    for d in (0, 2, 1):
+        g2s[d].wait_recv()
+        for i, (taps, target) in enumerate(((pl.ds(0, 5), z_next), (pl.ds(5, 4), z_prev))):
+            part = quarter(w2, lax.rem(x + 3 - d, 4), taps)
+            c = remote(part, part, wzs.at[2 * d + i], wzr.at[2 * d + i], target)
+            c.start()
+            by_z.append(c)
+
     for c in f1:
         c.wait()
     for d in range(3):
@@ -350,23 +359,20 @@
     hact_u.start()
     hact_d = remote(actr.at[8:12], actr.at[0:4], hs.at[19], hr.at[19], down)
     hact_d.start()
-    by_z = []
-    for d in (0, 2, 1):
-        g2s[d].wait_recv()
-        for i, (taps, target) in enumerate(((pl.ds(0, 5), z_next), (pl.ds(5, 4), z_prev))):
-            part = quarter(w2, lax.rem(x + 3 - d, 4), taps)
-            c = remote(part, part, wzs.at[2 * d + i], wzr.at[2 * d + i], target)
-            c.start()
-            by_z.append(c)
-    f2 = []
-    for i, d in enumerate((0, 2, 1)):
-        by_z[2 * i].wait_recv()
-        by_z[2 * i + 1].wait_recv()
-        f2.append(hand_on(w2, d, every, 3))
-    lw2.wait()
 
     yc1 = []
+    def second_on():
+        f2 = []
+        for i, d in enumerate((0, 2, 1)):
+            by_z[2 * i].wait_recv()
+            by_z[2 * i + 1].wait_recv()
+            f2.append(hand_on(w2, d, every, 3))
+        lw2.wait()
+        return f2
+
     for chunk in range(4):
+        if chunk == 2:
+            f2 = second_on()
         for c in xc1[3 * chunk : 3 * chunk + 3]:
             c.wait()
         for j in (2 * chunk, 2 * chunk + 1):

time: 50.7 us -> 48.3 us (0.953)
  Pallas kernels: 50 us -> 47.2 us
    pallas_call x1, Pallas kernels: 48.9 us -> 46.1 us  [body(): pl.pallas_call(kernel, name='section', out_shape=(pltpu.VMEM((8, 64, 256)...]
where the time goes in v5:
time: 48.3 us; the launch traced here: 47.8 us
  Pallas kernels  47.2 us (98%)
  between operations  0.64 us (1%)
    pallas_call x1, Pallas kernels, body(): pl.pallas_call(kernel, name='section', out_shape=(pltpu.VMEM((8, 64, 256)...  46.1 us
    pallas_call x1, Pallas kernels, body(): pl.pallas_call(closing, name='closing', out_shape=(jax.ShapeDtypeStruct((...  1.08 us

profile of v5, /device:TPU:1, one launch (start us, length us, event | category | flops | bytes accessed | tf_op | source)
XLA Modules:
  0.0 47.8 jit_solution(2720588047199745069)
XLA Ops:
  0.6 46.1 %section.1 = (bf16[8,64,256]{2,1,0:T(8,128)(2,1)S(1)}, bf16[16,128,256]{2,1,0:T(8,128)(2,1)S(1)}, f32[1152]{0:T(1024)S(1)}) custom-call(bf16[16,128,256]{2,1,0:T(8,128)(2,1)} %bitcast.6, bf16[9,64,256]{2,1,0:T(8,128)(2,1)} %bitcast.7, bf16[9,64,256]{2,1,0:T(8,128)(2,1)} %bitcast.8, bf16[8,64,256]{2,1,0:T(8,128)(2,1)} %bitcast.9), custom_call_target="tpu_custom_call" | custom-call | tf_op jit(solution)/shard_map/section/pallas_call | solution.py:589
  46.8 1.1 %closing.1 = (bf16[8,64,256]{2,1,0:T(8,128)(2,1)}, bf16[16,128,256]{2,1,0:T(8,128)(2,1)}, f32[1152]{0:T(1024)}) custom-call(bf16[8,64,256]{2,1,0:T(8,128)(2,1)S(1)} %get-tuple-element.9.enc_in, bf16[16,128,256]{2,1,0:T(8,128)(2,1)S(1)} %get-tuple-element.10.ing_in, f32[1152]{0:T(1024)S(1)} %get-tuple-element.11.kg_in), custom_call_target="tpu_custom_call" | custom-call | tf_op jit(solution)/shard_map/closing/pallas_call | solution.py:609
